TPU v7x, 256 devices: a whole 4x4x8 slice. The times are simulated.
256 devices in a mesh: slab: 64 (over y, z, core), grp: 4 (over x).
Axes of the slice: x: 4, y: 4, z: 8, core: 2. Of those that a mesh axis runs over, the one named last changes fastest.
Arguments:
- surf_pos: float32 [3, 1048576], P(None, ('slab', 'grp')), may hold values from -1 to 1
- surf_motion: float32 [7, 1048576], P(None, ('slab', 'grp')), may hold values from -6 to 6
- surf_bin: int32 [1048576], P(('slab', 'grp')), may hold values from 0 to 255, as said below
- vol_pos: float32 [3, 262144], P(None, ('slab', 'grp')), may hold values from -1 to 1
- influence: int32 [256, 8], P(('slab', 'grp')), may hold values from 0 to 255, as said below
- list_count: int32 [256], P(('slab', 'grp')), may hold values from 2 to 8
Outputs:
- vol_motion: float32 [7, 262144], P(None, ('slab', 'grp'))
Inputs may be any that keep to these rules, and one draw needn't show every extreme that they name: `surf_bin`: A node on the device at place d = s * 4 + g of the slab+grp order has a bin of the form t * 4 + g; each device gives exactly 64 of its nodes to each slab t, so every bin holds 4096 nodes. `influence`: row d = s * 4 + g holds 8 distinct bin ids b with |b // 4 - s| <= 2; only the first list_count[d] are used.
All inputs are finite; a program needn't handle non-finite values.
Results may differ from a plain program's by a relative error of at most 0.0003.
Values sent between devices are 32-bit elements; how exact they have to be, the bound alone decides.
A program may use at most 128 MiB of HBM per device.

v0:
```python
import jax
import jax.numpy as jnp
from jax import lax
from jax.sharding import PartitionSpec as P

REACH = 2


def passed_along(block, axis, distance):
    devices = range(lax.axis_size(axis))
    route = [(i - distance, i) for i in devices if i - distance in devices]
    return lax.ppermute(block, axis, route)


def blend_rows(vol, pos, mot):
    r2 = (vol[0][:, None] - pos[0][None, :]) ** 2
    r2 = r2 + (vol[1][:, None] - pos[1][None, :]) ** 2
    r2 = r2 + (vol[2][:, None] - pos[2][None, :]) ** 2
    inverse = 1.0 / (r2 + 0.01)
    weight = inverse * inverse
    numer = jnp.einsum("cb,vb->cv", mot, weight, precision=lax.Precision.HIGHEST)
    return (numer, jnp.sum(weight, axis=1))


def blend(vol, pos, mot):
    count = vol.shape[1]
    rows = min(512, count)
    blocks = count // rows
    pieces = vol.reshape(3, blocks, rows).transpose(1, 0, 2)
    numer, denom = lax.map(lambda piece: blend_rows(piece, pos, mot), pieces)
    return (numer.transpose(1, 0, 2).reshape(7, count), denom.reshape(count))


def on_device(surf_pos, surf_motion, surf_bin, vol_pos, influence, list_count):
    nslab = lax.axis_size("slab")
    ngrp = lax.axis_size("grp")
    width = surf_pos.shape[1]
    span = width // nslab
    nvol = vol_pos.shape[1]
    order = jnp.argsort(surf_bin // ngrp, stable=True)
    send_pos = surf_pos[:, order].reshape(3, nslab, span)
    send_mot = surf_motion[:, order].reshape(7, nslab, span)
    own_pos, own_mot = (
        lax.all_to_all(send_pos, "slab", split_axis=1, concat_axis=1, tiled=True),
        lax.all_to_all(send_mot, "slab", split_axis=1, concat_axis=1, tiled=True),
    )
    own_pos = own_pos.reshape(3, width)
    own_mot = own_mot.reshape(7, width)
    slab_index = lax.axis_index("slab")
    offsets = [step for level in range(1, REACH + 1) for step in (level, -level)]
    zero_num = jnp.zeros((7, nvol), jnp.float32)
    zero_den = jnp.zeros((nvol,), jnp.float32)
    group = (
        lax.all_gather(own_pos[None], "grp", axis=0, tiled=True),
        lax.all_gather(own_mot[None], "grp", axis=0, tiled=True),
    )
    window = {0: group}
    for by in offsets:
        window[-by] = passed_along((group[0], group[1]), "slab", by)
    all_pos = jnp.stack([window[rel][0] for rel in range(-REACH, REACH + 1)])
    all_mot = jnp.stack([window[rel][1] for rel in range(-REACH, REACH + 1)])
    row = influence[0]

    def step(index, carry):
        numer, denom = carry
        bin_id = row[index]
        rel_index = bin_id // ngrp - slab_index + REACH
        member = bin_id % ngrp
        extra_num, extra_den = blend(
            vol_pos, all_pos[rel_index, member], all_mot[rel_index, member]
        )
        return (numer + extra_num, denom + extra_den)

    numer, denom = lax.fori_loop(0, list_count[0], step, (zero_num, zero_den))
    return numer / denom[None, :]


def solution(mesh):
    return jax.shard_map(
        on_device,
        mesh=mesh,
        in_specs=(
            P(None, ("slab", "grp")),
            P(None, ("slab", "grp")),
            P(("slab", "grp")),
            P(None, ("slab", "grp")),
            P(("slab", "grp"), None),
            P(("slab", "grp")),
        ),
        out_specs=P(None, ("slab", "grp")),
        check_vma=False,
    )
```

profile of v0, /device:TPU:14, one launch (start us, length us, event | category | flops | bytes accessed | tf_op | source)
XLA Modules:
  0.0 410.7 jit_solution(2669482878264697277)
XLA Ops:
  8.0 14.2 %gather_fusion = f32[4096,3]{1,0:T(8,128)} fusion(f32[3,4096]{0,1:T(8,128)S(1)} %copy.21, s32[4096]{0:T(1024)S(1)} %fusion.7), kind=kCustom, calls=%fused_computation | custom fusion | bytes 114688 | tf_op jit(solution)/shard_map/gather | solution.py:41
  25.3 12.1 %all-to-all-start = ((f32[64,1,192]{2,1,0:T(1,128)}), f32[64,1,192]{2,1,0:T(1,128)S(1)}, u32[]{:S(2)}, u32[]{:S(2)}) async-start(f32[64,1,192]{2,1,0:T(1,128)} %reshape.54), calls=%async_computation | async-start | bytes 131072 | tf_op jit(solution)/shard_map/all_to_all | solution.py:44
  38.0 14.2 %gather_fusion.1 = f32[4096,7]{1,0:T(8,128)} fusion(f32[7,4096]{0,1:T(8,128)S(1)} %copy.24, s32[4096]{0:T(1024)S(1)} %fusion.7), kind=kCustom, calls=%fused_computation.1 | custom fusion | bytes 245760 | tf_op jit(solution)/shard_map/gather | solution.py:42
  55.3 10.3 %all-to-all-start.1 = ((f32[64,1,448]{2,1,0:T(1,128)}), f32[64,1,448]{2,1,0:T(1,128)S(1)}, u32[]{:S(2)}, u32[]{:S(2)}) async-start(f32[64,1,448]{2,1,0:T(1,128)} %reshape.56), calls=%async_computation.1 | async-start | bytes 262144 | tf_op jit(solution)/shard_map/all_to_all | solution.py:45
  67.2 12.3 %all_gather.6 = f32[4,3,4096]{2,1,0:T(4,128)S(1)} all-gather(f32[1,3,4096]{2,1,0:T(4,128)S(1)} %broadcast_in_dim_reshape.6), channel_id=1, replica_groups=mesh['slab'=64,'grp'=4] {'grp'}, dimensions={0}, use_global_device_ids=true | all-gather | bytes 245760 | tf_op jit(solution)/shard_map/all_gather | solution.py:54
  94.2 13.3 %all_gather.7 = f32[4,7,4096]{2,1,0:T(8,128)S(1)} all-gather(f32[1,7,4096]{2,1,0:T(8,128)S(1)} %broadcast_in_dim_reshape.7), channel_id=1, replica_groups=mesh['slab'=64,'grp'=4] {'grp'}, dimensions={0}, use_global_device_ids=true | all-gather | bytes 573440 | tf_op jit(solution)/shard_map/all_gather | solution.py:55
  136.1 274.0 %while.39 = (s32[]{:T(128)}, f32[7,1024]{1,0:T(8,128)S(1)}, f32[1024]{0:T(1024)S(1)}, s32[]{:T(128)}, f32[3,1024]{1,0:T(4,128)}, /*index=5*/s32[8]{0:T(128)S(1)}...) while((s32[]{:T(128)}, f32[7,1024]{1,0:T(8,128)S(1)}, ...), condition=%wide.region_5.6_spmd, body=%wide.region_1.5_spmd.sunk | while | flops 224402976 | bytes 809723 | solution.py:74
  141.1 29.3 %while.40 = (s32[]{:T(128)}, f32[2,7,512]{2,1,0:T(8,128)S(1)}, f32[2,512]{1,0:T(2,128)S(1)}, f32[2,3,512]{2,1,0:T(4,128)}, f32[3,4096]{1,0:T(4,128)S(1)}, /*inde...) while((s32[]{:T(128)}, f32[2,7,512]{2,1,0:T(8,128)S(1)}, f32[2,512]{1,0:T(2,128)S(1)}, ...), condition=%wide.region_4.4_spmd, body=%wide.region_2.3_spmd.sunk | while | flops 224394752 | bytes 374929 | solution.py:30
  142.0 10.1 %fusion.17 = f32[2,7,512]{2,1,0:T(8,128)S(1)} fusion(f32[2,7,512]{2,1,0:T(8,128)S(1)} %get-tuple-element.332, s32[]{:T(128)} %get-tuple-element.331, f32[7,4096]{1,0:T(8,128)S(1)} %get-tuple-element.346, f32[4096]{0:T(1024)S(1)} %bitcast.93, f32[512]{0:T(512)S(1)} %bitcast.105, f32[4096]{0:T(1024)S(1)} %bitcast.95, f32[512]{0:T(512)S(1)} %bitcast.103, ...), kind=kOutput, calls=%fused_computation.6.clone.1 | convolution fusion | flops 199229440 | bytes 202756 | tf_op jit(solution)/shard_map/while/body/while/body/eval_jaxpr/cb,vb->cv/dot_general | solution.py:21
  156.6 10.1 %fusion.17 = f32[2,7,512]{2,1,0:T(8,128)S(1)} fusion(f32[2,7,512]{2,1,0:T(8,128)S(1)} %get-tuple-element.332, s32[]{:T(128)} %get-tuple-element.331, f32[7,4096]{1,0:T(8,128)S(1)} %get-tuple-element.346, f32[4096]{0:T(1024)S(1)} %bitcast.93, f32[512]{0:T(512)S(1)} %bitcast.105, f32[4096]{0:T(1024)S(1)} %bitcast.95, f32[512]{0:T(512)S(1)} %bitcast.103, ...), kind=kOutput, calls=%fused_computation.6.clone.1 | convolution fusion | flops 199229440 | bytes 202756 | tf_op jit(solution)/shard_map/while/body/while/body/eval_jaxpr/cb,vb->cv/dot_general | solution.py:21
  175.3 29.3 %while.40 = (s32[]{:T(128)}, f32[2,7,512]{2,1,0:T(8,128)S(1)}, f32[2,512]{1,0:T(2,128)S(1)}, f32[2,3,512]{2,1,0:T(4,128)}, f32[3,4096]{1,0:T(4,128)S(1)}, /*inde...) while((s32[]{:T(128)}, f32[2,7,512]{2,1,0:T(8,128)S(1)}, f32[2,512]{1,0:T(2,128)S(1)}, ...), condition=%wide.region_4.4_spmd, body=%wide.region_2.3_spmd.sunk | while | flops 224394752 | bytes 374929 | solution.py:30
  176.1 10.1 %fusion.17 = f32[2,7,512]{2,1,0:T(8,128)S(1)} fusion(f32[2,7,512]{2,1,0:T(8,128)S(1)} %get-tuple-element.332, s32[]{:T(128)} %get-tuple-element.331, f32[7,4096]{1,0:T(8,128)S(1)} %get-tuple-element.346, f32[4096]{0:T(1024)S(1)} %bitcast.93, f32[512]{0:T(512)S(1)} %bitcast.105, f32[4096]{0:T(1024)S(1)} %bitcast.95, f32[512]{0:T(512)S(1)} %bitcast.103, ...), kind=kOutput, calls=%fused_computation.6.clone.1 | convolution fusion | flops 199229440 | bytes 202756 | tf_op jit(solution)/shard_map/while/body/while/body/eval_jaxpr/cb,vb->cv/dot_general | solution.py:21
  190.8 10.1 %fusion.17 = f32[2,7,512]{2,1,0:T(8,128)S(1)} fusion(f32[2,7,512]{2,1,0:T(8,128)S(1)} %get-tuple-element.332, s32[]{:T(128)} %get-tuple-element.331, f32[7,4096]{1,0:T(8,128)S(1)} %get-tuple-element.346, f32[4096]{0:T(1024)S(1)} %bitcast.93, f32[512]{0:T(512)S(1)} %bitcast.105, f32[4096]{0:T(1024)S(1)} %bitcast.95, f32[512]{0:T(512)S(1)} %bitcast.103, ...), kind=kOutput, calls=%fused_computation.6.clone.1 | convolution fusion | flops 199229440 | bytes 202756 | tf_op jit(solution)/shard_map/while/body/while/body/eval_jaxpr/cb,vb->cv/dot_general | solution.py:21
  209.4 29.3 %while.40 = (s32[]{:T(128)}, f32[2,7,512]{2,1,0:T(8,128)S(1)}, f32[2,512]{1,0:T(2,128)S(1)}, f32[2,3,512]{2,1,0:T(4,128)}, f32[3,4096]{1,0:T(4,128)S(1)}, /*inde...) while((s32[]{:T(128)}, f32[2,7,512]{2,1,0:T(8,128)S(1)}, f32[2,512]{1,0:T(2,128)S(1)}, ...), condition=%wide.region_4.4_spmd, body=%wide.region_2.3_spmd.sunk | while | flops 224394752 | bytes 374929 | solution.py:30
  210.3 10.1 %fusion.17 = f32[2,7,512]{2,1,0:T(8,128)S(1)} fusion(f32[2,7,512]{2,1,0:T(8,128)S(1)} %get-tuple-element.332, s32[]{:T(128)} %get-tuple-element.331, f32[7,4096]{1,0:T(8,128)S(1)} %get-tuple-element.346, f32[4096]{0:T(1024)S(1)} %bitcast.93, f32[512]{0:T(512)S(1)} %bitcast.105, f32[4096]{0:T(1024)S(1)} %bitcast.95, f32[512]{0:T(512)S(1)} %bitcast.103, ...), kind=kOutput, calls=%fused_computation.6.clone.1 | convolution fusion | flops 199229440 | bytes 202756 | tf_op jit(solution)/shard_map/while/body/while/body/eval_jaxpr/cb,vb->cv/dot_general | solution.py:21
  224.9 10.1 %fusion.17 = f32[2,7,512]{2,1,0:T(8,128)S(1)} fusion(f32[2,7,512]{2,1,0:T(8,128)S(1)} %get-tuple-element.332, s32[]{:T(128)} %get-tuple-element.331, f32[7,4096]{1,0:T(8,128)S(1)} %get-tuple-element.346, f32[4096]{0:T(1024)S(1)} %bitcast.93, f32[512]{0:T(512)S(1)} %bitcast.105, f32[4096]{0:T(1024)S(1)} %bitcast.95, f32[512]{0:T(512)S(1)} %bitcast.103, ...), kind=kOutput, calls=%fused_computation.6.clone.1 | convolution fusion | flops 199229440 | bytes 202756 | tf_op jit(solution)/shard_map/while/body/while/body/eval_jaxpr/cb,vb->cv/dot_general | solution.py:21
  243.5 29.3 %while.40 = (s32[]{:T(128)}, f32[2,7,512]{2,1,0:T(8,128)S(1)}, f32[2,512]{1,0:T(2,128)S(1)}, f32[2,3,512]{2,1,0:T(4,128)}, f32[3,4096]{1,0:T(4,128)S(1)}, /*inde...) while((s32[]{:T(128)}, f32[2,7,512]{2,1,0:T(8,128)S(1)}, f32[2,512]{1,0:T(2,128)S(1)}, ...), condition=%wide.region_4.4_spmd, body=%wide.region_2.3_spmd.sunk | while | flops 224394752 | bytes 374929 | solution.py:30
  244.4 10.1 %fusion.17 = f32[2,7,512]{2,1,0:T(8,128)S(1)} fusion(f32[2,7,512]{2,1,0:T(8,128)S(1)} %get-tuple-element.332, s32[]{:T(128)} %get-tuple-element.331, f32[7,4096]{1,0:T(8,128)S(1)} %get-tuple-element.346, f32[4096]{0:T(1024)S(1)} %bitcast.93, f32[512]{0:T(512)S(1)} %bitcast.105, f32[4096]{0:T(1024)S(1)} %bitcast.95, f32[512]{0:T(512)S(1)} %bitcast.103, ...), kind=kOutput, calls=%fused_computation.6.clone.1 | convolution fusion | flops 199229440 | bytes 202756 | tf_op jit(solution)/shard_map/while/body/while/body/eval_jaxpr/cb,vb->cv/dot_general | solution.py:21
  259.1 10.1 %fusion.17 = f32[2,7,512]{2,1,0:T(8,128)S(1)} fusion(f32[2,7,512]{2,1,0:T(8,128)S(1)} %get-tuple-element.332, s32[]{:T(128)} %get-tuple-element.331, f32[7,4096]{1,0:T(8,128)S(1)} %get-tuple-element.346, f32[4096]{0:T(1024)S(1)} %bitcast.93, f32[512]{0:T(512)S(1)} %bitcast.105, f32[4096]{0:T(1024)S(1)} %bitcast.95, f32[512]{0:T(512)S(1)} %bitcast.103, ...), kind=kOutput, calls=%fused_computation.6.clone.1 | convolution fusion | flops 199229440 | bytes 202756 | tf_op jit(solution)/shard_map/while/body/while/body/eval_jaxpr/cb,vb->cv/dot_general | solution.py:21
  277.7 29.3 %while.40 = (s32[]{:T(128)}, f32[2,7,512]{2,1,0:T(8,128)S(1)}, f32[2,512]{1,0:T(2,128)S(1)}, f32[2,3,512]{2,1,0:T(4,128)}, f32[3,4096]{1,0:T(4,128)S(1)}, /*inde...) while((s32[]{:T(128)}, f32[2,7,512]{2,1,0:T(8,128)S(1)}, f32[2,512]{1,0:T(2,128)S(1)}, ...), condition=%wide.region_4.4_spmd, body=%wide.region_2.3_spmd.sunk | while | flops 224394752 | bytes 374929 | solution.py:30
  278.6 10.1 %fusion.17 = f32[2,7,512]{2,1,0:T(8,128)S(1)} fusion(f32[2,7,512]{2,1,0:T(8,128)S(1)} %get-tuple-element.332, s32[]{:T(128)} %get-tuple-element.331, f32[7,4096]{1,0:T(8,128)S(1)} %get-tuple-element.346, f32[4096]{0:T(1024)S(1)} %bitcast.93, f32[512]{0:T(512)S(1)} %bitcast.105, f32[4096]{0:T(1024)S(1)} %bitcast.95, f32[512]{0:T(512)S(1)} %bitcast.103, ...), kind=kOutput, calls=%fused_computation.6.clone.1 | convolution fusion | flops 199229440 | bytes 202756 | tf_op jit(solution)/shard_map/while/body/while/body/eval_jaxpr/cb,vb->cv/dot_general | solution.py:21
  311.8 29.3 %while.40 = (s32[]{:T(128)}, f32[2,7,512]{2,1,0:T(8,128)S(1)}, f32[2,512]{1,0:T(2,128)S(1)}, f32[2,3,512]{2,1,0:T(4,128)}, f32[3,4096]{1,0:T(4,128)S(1)}, /*inde...) while((s32[]{:T(128)}, f32[2,7,512]{2,1,0:T(8,128)S(1)}, f32[2,512]{1,0:T(2,128)S(1)}, ...), condition=%wide.region_4.4_spmd, body=%wide.region_2.3_spmd.sunk | while | flops 224394752 | bytes 374929 | solution.py:30
  346.0 29.3 %while.40 = (s32[]{:T(128)}, f32[2,7,512]{2,1,0:T(8,128)S(1)}, f32[2,512]{1,0:T(2,128)S(1)}, f32[2,3,512]{2,1,0:T(4,128)}, f32[3,4096]{1,0:T(4,128)S(1)}, /*inde...) while((s32[]{:T(128)}, f32[2,7,512]{2,1,0:T(8,128)S(1)}, f32[2,512]{1,0:T(2,128)S(1)}, ...), condition=%wide.region_4.4_spmd, body=%wide.region_2.3_spmd.sunk | while | flops 224394752 | bytes 374929 | solution.py:30
  380.1 29.3 %while.40 = (s32[]{:T(128)}, f32[2,7,512]{2,1,0:T(8,128)S(1)}, f32[2,512]{1,0:T(2,128)S(1)}, f32[2,3,512]{2,1,0:T(4,128)}, f32[3,4096]{1,0:T(4,128)S(1)}, /*inde...) while((s32[]{:T(128)}, f32[2,7,512]{2,1,0:T(8,128)S(1)}, f32[2,512]{1,0:T(2,128)S(1)}, ...), condition=%wide.region_4.4_spmd, body=%wide.region_2.3_spmd.sunk | while | flops 224394752 | bytes 374929 | solution.py:30
  (191 shorter events, 216.1 us)
Async XLA Ops:
  6.5 30.8 %copy-start.1 = (f32[7,4096]{1,0:T(8,128)S(1)}, f32[7,4096]{1,0:T(8,128)}, u32[]{:S(2)}) copy-start(f32[7,4096]{1,0:T(8,128)} %param.11) | copy-start | bytes 344068
  25.3 30.1 %all-to-all-start = ((f32[64,1,192]{2,1,0:T(1,128)}), f32[64,1,192]{2,1,0:T(1,128)S(1)}, u32[]{:S(2)}, u32[]{:S(2)}) async-start(f32[64,1,192]{2,1,0:T(1,128)} %reshape.54), calls=%async_computation | async-start | bytes 131072 | tf_op jit(solution)/shard_map/all_to_all | solution.py:44
  55.3 37.7 %all-to-all-start.1 = ((f32[64,1,448]{2,1,0:T(1,128)}), f32[64,1,448]{2,1,0:T(1,128)S(1)}, u32[]{:S(2)}, u32[]{:S(2)}) async-start(f32[64,1,448]{2,1,0:T(1,128)} %reshape.56), calls=%async_computation.1 | async-start | bytes 262144 | tf_op jit(solution)/shard_map/all_to_all | solution.py:45
  79.5 30.9 %collective-permute-start = (f32[4,3,4096]{2,1,0:T(4,128)S(1)}, f32[4,3,4096]{2,1,0:T(4,128)S(1)}, u32[]{:S(2)}, u32[]{:S(2)}) collective-permute-start(f32[4,3,4096]{2,1,0:T(4,128)S(1)} %all_gather.6), channel_id=1, source_target_pairs={{0,8},{4,12},{8,16},{12,20},{16,24},{20,28},{24,32},{28,36},{32,40... | collective-permute-start | bytes 589832 | tf_op jit(solution)/shard_map/ppermute | solution.py:12
  82.8 29.5 %collective-permute-start.1 = (f32[4,3,4096]{2,1,0:T(4,128)S(1)}, f32[4,3,4096]{2,1,0:T(4,128)S(1)}, u32[]{:S(2)}, u32[]{:S(2)}) collective-permute-start(f32[4,3,4096]{2,1,0:T(4,128)S(1)} %all_gather.6), channel_id=1, source_target_pairs={{0,4},{4,8},{8,12},{12,16},{16,20},{20,24},{24,28},{28,32},{32,36}... | collective-permute-start | bytes 589832 | tf_op jit(solution)/shard_map/ppermute | solution.py:12
  84.8 33.5 %collective-permute-start.2 = (f32[4,3,4096]{2,1,0:T(4,128)S(1)}, f32[4,3,4096]{2,1,0:T(4,128)S(1)}, u32[]{:S(2)}, u32[]{:S(2)}) collective-permute-start(f32[4,3,4096]{2,1,0:T(4,128)S(1)} %all_gather.6), channel_id=1, source_target_pairs={{4,0},{8,4},{12,8},{16,12},{20,16},{24,20},{28,24},{32,28},{36,32}... | collective-permute-start | bytes 589832 | tf_op jit(solution)/shard_map/ppermute | solution.py:12
  90.5 30.9 %collective-permute-start.3 = (f32[4,3,4096]{2,1,0:T(4,128)S(1)}, f32[4,3,4096]{2,1,0:T(4,128)S(1)}, u32[]{:S(2)}, u32[]{:S(2)}) collective-permute-start(f32[4,3,4096]{2,1,0:T(4,128)S(1)} %all_gather.6), channel_id=1, source_target_pairs={{8,0},{12,4},{16,8},{20,12},{24,16},{28,20},{32,24},{36,28},{40,32... | collective-permute-start | bytes 589832 | tf_op jit(solution)/shard_map/ppermute | solution.py:12
  107.6 18.0 %collective-permute-start.4 = (f32[4,7,4096]{2,1,0:T(8,128)S(1)}, f32[4,7,4096]{2,1,0:T(8,128)S(1)}, u32[]{:S(2)}, u32[]{:S(2)}) collective-permute-start(f32[4,7,4096]{2,1,0:T(8,128)S(1)} %all_gather.7), channel_id=1, source_target_pairs={{0,8},{4,12},{8,16},{12,20},{16,24},{20,28},{24,32},{28,36},{32,40... | collective-permute-start | bytes 1376264 | tf_op jit(solution)/shard_map/ppermute | solution.py:12
  110.4 16.7 %collective-permute-start.5 = (f32[4,7,4096]{2,1,0:T(8,128)S(1)}, f32[4,7,4096]{2,1,0:T(8,128)S(1)}, u32[]{:S(2)}, u32[]{:S(2)}) collective-permute-start(f32[4,7,4096]{2,1,0:T(8,128)S(1)} %all_gather.7), channel_id=1, source_target_pairs={{0,4},{4,8},{8,12},{12,16},{16,20},{20,24},{24,28},{28,32},{32,36}... | collective-permute-start | bytes 1376264 | tf_op jit(solution)/shard_map/ppermute | solution.py:12
  112.4 16.5 %collective-permute-start.6 = (f32[4,7,4096]{2,1,0:T(8,128)S(1)}, f32[4,7,4096]{2,1,0:T(8,128)S(1)}, u32[]{:S(2)}, u32[]{:S(2)}) collective-permute-start(f32[4,7,4096]{2,1,0:T(8,128)S(1)} %all_gather.7), channel_id=1, source_target_pairs={{4,0},{8,4},{12,8},{16,12},{20,16},{24,20},{28,24},{32,28},{36,32}... | collective-permute-start | bytes 1376264 | tf_op jit(solution)/shard_map/ppermute | solution.py:12
  118.3 17.8 %collective-permute-start.7 = (f32[4,7,4096]{2,1,0:T(8,128)S(1)}, f32[4,7,4096]{2,1,0:T(8,128)S(1)}, u32[]{:S(2)}, u32[]{:S(2)}) collective-permute-start(f32[4,7,4096]{2,1,0:T(8,128)S(1)} %all_gather.7), channel_id=1, source_target_pairs={{8,0},{12,4},{16,8},{20,12},{24,16},{28,20},{32,24},{36,28},{40,32... | collective-permute-start | bytes 1376264 | tf_op jit(solution)/shard_map/ppermute | solution.py:12
  121.5 1.1 copy-start
  122.6 13.6 %copy-start.2 = (s32[1,8]{1,0:T(1,128)S(1)}, s32[1,8]{1,0:T(1,128)}, u32[]{:S(2)}) copy-start(s32[1,8]{1,0:T(1,128)} %param.14) | copy-start | bytes 100
where the time goes:
time: 413 us; the launch traced here: 411 us
  matrix products  161 us (39%)
  other arithmetic  67.9 us (16%)
  local copies, waits for them, and re-layouts  65.8 us (16%)
  starting transfers between devices  49.4 us (12%)
  loops' own time  27.5 us (7%)
  blocking collectives  25.6 us (6%)
  waiting for transfers between devices  13.4 us (3%)
    dot_general x16, matrix products, blend_rows(): jnp.einsum('cb,vb->cv', mot, weight, precision=lax.Precision.HIGHEST)  161 us
    reduce_sum x16, other arithmetic, blend_rows(): return (numer, jnp.sum(weight, axis=1))  58.9 us
    another operation x1, loops' own time, on_device(): numer, denom = lax.fori_loop(0, list_count[0], step, (zero_num, zero_den))  27.2 us
    ppermute x8, starting transfers between devices, passed_along(): return lax.ppermute(block, axis, route)  27 us
    gather x1, local copies, waits for them, and re-layouts, on_device(): send_pos = surf_pos[:, order].reshape(3, nslab, span)  14.2 us
    gather x1, local copies, waits for them, and re-layouts, on_device(): send_mot = surf_motion[:, order].reshape(7, nslab, span)  14.2 us
    slice x32, local copies, waits for them, and re-layouts, blend_rows(): r2 = (vol[0][:, None] - pos[0][None, :]) ** 2  13.7 us
    ppermute x8, waiting for transfers between devices, passed_along(): return lax.ppermute(block, axis, route)  13.3 us
  transfers between devices with their start and end apart: 10, of which 4 were waited for; matrix products, arithmetic and copies ran while one was open for 5% of the time, Pallas kernels for 0%

commit v1 on v0

v1 whole, which is shorter than its diff:
```python
import functools

import jax
import jax.numpy as jnp
from jax import lax
from jax.experimental import pallas as pl
from jax.experimental.pallas import tpu as pltpu
from jax.sharding import PartitionSpec as P

F32, BF16 = jnp.float32, jnp.bfloat16
MESH = pl.DeviceIdType.MESH
VMEM = pl.BlockSpec(memory_space=pltpu.VMEM)
SMEM = pl.BlockSpec(memory_space=pltpu.SMEM)
ROWS = 16
LANES = 128
CORES = 2


def dot(a, b):
    return lax.dot_general(a, b, (((1,), (0,)), ((), ())), preferred_element_type=F32)


def split3(x):
    first = x.astype(BF16).astype(F32)
    rest = x - first
    second = rest.astype(BF16).astype(F32)
    return first, second, (rest - second).astype(BF16).astype(F32)


def place():
    slab = lax.axis_index("slab")
    return slab // CORES, slab % CORES, lax.axis_index("grp")


def peer_of(me, offset, ngrp):
    other = (me + offset) % (CORES * ngrp)
    return other // ngrp, other % ngrp


def exchange_kernel(nchip, ngrp, pos, mot, bins, vol, infl, cnt, win, vols, lists,
                    xs, dcol, send, a_send, a_recv, f_send, f_recv, v_send, v_recv, l_send, l_recv):
    q, c, x = place()
    nz = nchip // ngrp
    blocks = bins.shape[0]
    nslab = nchip * CORES
    span = LANES // CORES
    members = CORES * ngrp
    me = c * ngrp + x
    up, down = (q + 1) % nchip, (q + nchip - 1) % nchip

    barrier = pltpu.get_barrier_semaphore()

    def greet(device):
        pl.semaphore_signal(barrier, inc=1, device_id=device, device_id_type=MESH)

    def greet_source(i, carry):
        greet((i * CORES + 1 - c, (x + ngrp - i // nz) % ngrp))
        return carry

    lax.fori_loop(0, nchip, greet_source, 0)
    greet((up * CORES + c, x))
    greet((down * CORES + c, x))
    for o in range(1, members):
        pc, px = peer_of(me, o, ngrp)
        greet((q * CORES + pc, px))

    vols[pl.ds(me, 1)] = vol[...][None]
    lane = lax.broadcasted_iota(jnp.int32, (1, LANES), 1)
    row = jnp.where(lane == infl.shape[1], cnt[0], 0)
    for l in range(infl.shape[1]):
        row = jnp.where(lane == l, infl[0, l], row)
    lists[pl.ds(me, 1)] = row[None]

    xs[...] = jnp.zeros_like(xs)
    xs[0:7, :] = mot[...]
    xs[8:11, :] = pos[...]
    slab_of = bins[...] // ngrp
    sub = lax.broadcasted_iota(jnp.int32, (nslab, LANES), 0)
    tri_r = lax.broadcasted_iota(jnp.int32, (LANES, 2 * LANES), 0)
    tri_c = lax.broadcasted_iota(jnp.int32, (LANES, 2 * LANES), 1)
    tri = jnp.where((tri_r <= tri_c), 1.0, 0.0).astype(BF16)
    carry = jnp.zeros((nslab, LANES), F32)
    for k in range(blocks):
        trow = slab_of[k : k + 1, :]
        hit = trow == sub
        cum = dot(jnp.where(hit, 1.0, 0.0).astype(BF16), tri)
        rank = jnp.sum(jnp.where(hit, cum[:, :LANES] + carry, 0.0), axis=0, keepdims=True)
        carry = carry + cum[:, LANES:]
        dest = trow.astype(F32) * span + (rank - 1.0)
        wide = jnp.broadcast_to(dest, (LANES, LANES)).T
        dcol[k * LANES : (k + 1) * LANES, :] = wide.astype(jnp.int32)

    pl.semaphore_wait(barrier, nchip + 2 + members - 1)

    for o in range(1, members):
        pc, px = peer_of(me, o, ngrp)
        pltpu.make_async_remote_copy(
            src_ref=vols.at[me], dst_ref=vols.at[me], send_sem=v_send.at[o], recv_sem=v_recv.at[o],
            device_id=(q * CORES + pc, px), device_id_type=MESH).start()
        pltpu.make_async_remote_copy(
            src_ref=lists.at[me], dst_ref=lists.at[me], send_sem=l_send.at[o], recv_sem=l_recv.at[o],
            device_id=(q * CORES + pc, px), device_id_type=MESH).start()

    slot = x * nz + q % nz
    step_lanes = 2 * LANES
    steps = nchip // 2
    lane2 = lax.broadcasted_iota(jnp.int32, (step_lanes, LANES), 1)

    def to_bin(i):
        return pltpu.make_async_remote_copy(
            src_ref=send.at[i], dst_ref=win.at[1, slot], send_sem=a_send.at[i], recv_sem=a_recv.at[slot],
            device_id=(i * CORES + 1 - c, (x + q // nz) % ngrp), device_id_type=MESH)

    def order(i, _):
        tile = (q // 2 + i) % steps
        acc = jnp.zeros((3 * ROWS, step_lanes), F32)
        for k in range(blocks // 2):
            cols = slice(k * step_lanes, (k + 1) * step_lanes)
            part = jnp.concatenate(split3(xs[:, cols]), axis=0).astype(BF16)
            d = dcol[cols, :] - tile * step_lanes
            one = jnp.concatenate(
                [jnp.where(d == lane2, 1.0, 0.0), jnp.where(d == lane2 + LANES, 1.0, 0.0)], axis=1).astype(BF16)
            acc = acc + dot(part, one)
        full = acc[:ROWS] + acc[ROWS : 2 * ROWS] + acc[2 * ROWS :]
        send[2 * tile] = full[:, :LANES]
        send[2 * tile + 1] = full[:, LANES:]
        to_bin(2 * tile).start()
        to_bin(2 * tile + 1).start()
        return 0

    lax.fori_loop(0, steps, order, 0)

    def forward(g, to):
        part = pl.ds(g * nz, nz)
        return pltpu.make_async_remote_copy(
            src_ref=win.at[1, part], dst_ref=win.at[0 if to == 0 else 2, part],
            send_sem=f_send.at[to, g], recv_sem=f_recv.at[to, g],
            device_id=((up if to == 0 else down) * CORES + c, x), device_id_type=MESH)

    for g in range(ngrp):
        def arrived(z, _, g=g):
            s = g * nz + z
            pltpu.make_async_remote_copy(
                src_ref=send.at[0], dst_ref=win.at[1, s], send_sem=a_send.at[0], recv_sem=a_recv.at[s],
                device_id=(q * CORES + 1 - c, x), device_id_type=MESH).wait_recv()
            return 0

        lax.fori_loop(0, nz, arrived, 0)
        forward(g, 0).start()
        forward(g, 1).start()

    def left(i, _):
        to_bin(i).wait_send()
        return 0

    lax.fori_loop(0, nchip, left, 0)
    for o in range(1, members):
        other = (me + members - o) % members
        pc, px = peer_of(me, o, ngrp)
        for ref, s_sem, r_sem in ((vols, v_send, v_recv), (lists, l_send, l_recv)):
            copy = pltpu.make_async_remote_copy(
                src_ref=ref.at[me], dst_ref=ref.at[other], send_sem=s_sem.at[o], recv_sem=r_sem.at[o],
                device_id=(q * CORES + pc, px), device_id_type=MESH)
            copy.wait_send()
            copy.wait_recv()
    for g in range(ngrp):
        for to in range(2):
            copy = forward(g, to)
            copy.wait_send()
            copy.wait_recv()


def exchange(nchip, ngrp, pos, mot, bins, vol, infl, cnt):
    members = CORES * ngrp
    nvol = vol.shape[1]
    width = pos.shape[1]
    dma = pltpu.SemaphoreType.DMA
    return pl.pallas_call(
        functools.partial(exchange_kernel, nchip, ngrp),
        out_shape=(
            jax.ShapeDtypeStruct((3, nchip, ROWS, LANES), F32),
            jax.ShapeDtypeStruct((members, 3, nvol), F32),
            jax.ShapeDtypeStruct((members, 1, LANES), jnp.int32),
        ),
        in_specs=[VMEM, VMEM, VMEM, VMEM, SMEM, SMEM],
        out_specs=(VMEM, VMEM, VMEM),
        scratch_shapes=[
            pltpu.VMEM((ROWS, width), F32),
            pltpu.VMEM((width, LANES), jnp.int32),
            pltpu.VMEM((nchip, ROWS, LANES), F32),
            dma((nchip,)), dma((nchip,)),
            dma((2, ngrp)), dma((2, ngrp)),
            dma((members,)), dma((members,)),
            dma((members,)), dma((members,)),
        ],
        compiler_params=pltpu.CompilerParams(collective_id=0, has_side_effects=True, vmem_limit_bytes=48 << 20),
    )(pos, mot, bins, vol, infl, cnt)


def blend_kernel(ngrp, lists, win, vols, part, fs, mt, fv, acc):
    q, _, _ = place()
    members, _, nvol = vols.shape
    lmax_at = 8
    nz = win.shape[1] // ngrp
    base = (q - 1) * CORES * ngrp

    lane = lax.broadcasted_iota(jnp.int32, (ROWS, LANES), 1) < LANES // 2
    sub = lax.broadcasted_iota(jnp.int32, (8, LANES), 0)

    def features(t):
        first, second, third = split3(t)
        return first, second, third

    def prepare(i, _):
        chip, g = i // ngrp, i % ngrp
        for k in range(nz // 2):
            a = win[chip, g * nz + 2 * k]
            b = win[chip, g * nz + 2 * k + 1]
            pair = (jnp.where(lane, a, pltpu.roll(b, LANES // 2, 1)),
                    jnp.where(lane, pltpu.roll(a, LANES // 2, 1), b))
            cols = slice(k * LANES, (k + 1) * LANES)
            for tt in range(CORES):
                n = (chip * CORES + tt) * ngrp + g
                m = jnp.where(sub == 7, 1.0, pair[tt][:8])
                m1, m2, _ = split3(m)
                mt[n, :, cols] = jnp.concatenate([m1, m2], axis=0).astype(BF16)
                p = pair[tt][8:]
                p2 = p * p
                norm = p2[0:1] + p2[1:2] + p2[2:3] + 0.01
                y = jnp.where(sub < 3, -2.0 * p, jnp.where(sub == 3, norm, jnp.where(sub == 4, 1.0, 0.0)))
                y1, y2, y3 = split3(y)
                wide = jnp.concatenate([y1, y2, y3, y1, y2, y1], axis=0)
                fs[n, cols, :] = wide.T.astype(BF16)
        return 0

    lax.fori_loop(0, 3 * ngrp, prepare, 0)

    def prepare_vol(j, _):
        v = vols[j]
        v2 = v * v
        norm = v2[0:1] + v2[1:2] + v2[2:3]
        ones = jnp.ones_like(norm)
        zero = jnp.zeros_like(norm)
        w1, w2, w3 = split3(jnp.concatenate([v, ones, norm, zero, zero, zero], axis=0))
        fv[j] = jnp.concatenate([w1, w1, w1, w2, w2, w3], axis=0).astype(BF16)
        return 0

    lax.fori_loop(0, members, prepare_vol, 0)

    def block(j, _):
        acc[...] = jnp.zeros_like(acc)

        def item(l, _):
            n = lists[j, 0, l] - base
            d2 = dot(fs[n], fv[j])
            w = pltpu.reciprocal(d2 * d2, approx=True)
            w1 = w.astype(BF16)
            w2 = (w - w1.astype(F32)).astype(BF16)
            m = mt[n]
            acc[...] += dot(m, w1) + dot(m, w2)
            return 0

        lax.fori_loop(0, lists[j, 0, lmax_at], item, 0)
        part[j] = acc[:8] + acc[8:]
        return 0

    lax.fori_loop(0, members, block, 0)


def blend(ngrp, lists, win, vols):
    members, _, nvol = vols.shape
    nbin = 3 * CORES * ngrp
    nodes = win.shape[1] // ngrp * LANES // CORES
    return pl.pallas_call(
        functools.partial(blend_kernel, ngrp),
        out_shape=jax.ShapeDtypeStruct((members, 8, nvol), F32),
        in_specs=[SMEM, VMEM, VMEM],
        out_specs=VMEM,
        scratch_shapes=[
            pltpu.VMEM((nbin, nodes, 48), BF16),
            pltpu.VMEM((nbin, 16, nodes), BF16),
            pltpu.VMEM((members, 48, nvol), BF16),
            pltpu.VMEM((16, nvol), F32),
        ],
        compiler_params=pltpu.CompilerParams(vmem_limit_bytes=48 << 20),
    )(lists, win, vols)


def combine_kernel(ngrp, part, out, got, s_sem, r_sem):
    q, c, x = place()
    members = CORES * ngrp
    me = c * ngrp + x
    barrier = pltpu.get_barrier_semaphore()
    for o in range(1, members):
        pc, px = peer_of(me, o, ngrp)
        pl.semaphore_signal(barrier, inc=1, device_id=(q * CORES + pc, px), device_id_type=MESH)
    pl.semaphore_wait(barrier, members - 1)
    copies = []
    for o in range(1, members):
        pc, px = peer_of(me, o, ngrp)
        copy = pltpu.make_async_remote_copy(
            src_ref=part.at[(me + o) % members], dst_ref=got.at[o], send_sem=s_sem.at[o], recv_sem=r_sem.at[o],
            device_id=(q * CORES + pc, px), device_id_type=MESH)
        copy.start()
        copies.append(copy)
    total = part[me]
    for o in range(1, members):
        copies[o - 1].wait_recv()
        total = total + got[o]
    out[...] = total[:7] / total[7:8]
    for copy in copies:
        copy.wait_send()


def combine(ngrp, part):
    members, _, nvol = part.shape
    return pl.pallas_call(
        functools.partial(combine_kernel, ngrp),
        out_shape=jax.ShapeDtypeStruct((7, nvol), F32),
        in_specs=[VMEM],
        out_specs=VMEM,
        scratch_shapes=[
            pltpu.VMEM((members, 8, nvol), F32),
            pltpu.SemaphoreType.DMA((members,)),
            pltpu.SemaphoreType.DMA((members,)),
        ],
        compiler_params=pltpu.CompilerParams(collective_id=1, has_side_effects=True, vmem_limit_bytes=48 << 20),
    )(part)


def on_device(surf_pos, surf_motion, surf_bin, vol_pos, influence, list_count):
    nchip = lax.axis_size("slab") // CORES
    ngrp = lax.axis_size("grp")
    bins = surf_bin.reshape(-1, LANES)
    win, vols, lists = exchange(nchip, ngrp, surf_pos, surf_motion, bins, vol_pos, influence, list_count)
    part = blend(ngrp, lists, win, vols)
    return combine(ngrp, part)


def solution(mesh):
    return jax.shard_map(
        on_device,
        mesh=mesh,
        in_specs=(
            P(None, ("slab", "grp")),
            P(None, ("slab", "grp")),
            P(("slab", "grp")),
            P(None, ("slab", "grp")),
            P(("slab", "grp"), None),
            P(("slab", "grp")),
        ),
        out_specs=P(None, ("slab", "grp")),
        check_vma=False,
    )
```

time: 413 us -> 84 us (0.20)
  the two profiles are of different devices: /device:TPU:14 before, /device:TPU:56 now
where the time goes in v1:
time: 84 us; the launch traced here: 83.7 us
  Pallas kernels  78.6 us (94%)
  local copies, waits for them, and re-layouts  4.44 us (5%)
    pallas_call x1, Pallas kernels, blend(): pl.pallas_call(functools.partial(blend_kernel, ngrp), out_shape=jax.Shape...  40.2 us
    pallas_call x1, Pallas kernels, exchange(): pl.pallas_call(functools.partial(exchange_kernel, nchip, ngrp), out_shape...  28.5 us
    pallas_call x1, Pallas kernels, combine(): pl.pallas_call(functools.partial(combine_kernel, ngrp), out_shape=jax.Sha...  9.84 us
    unnamed x11, local copies, waits for them, and re-layouts  4.44 us

profile of v1, /device:TPU:56, one launch (start us, length us, event | category | flops | bytes accessed | tf_op | source)
XLA Modules:
  0.0 83.7 jit_solution(13952793127690955056)
XLA Ops:
  0.7 0.0 copy-start.4
  0.7 0.6 copy-done.4
  1.3 0.0 copy-start
  1.3 0.9 %copy-done = f32[7,4096]{1,0:T(8,128)S(1)} copy-done((f32[7,4096]{1,0:T(8,128)S(1)}, f32[7,4096]{1,0:T(8,128)}, u32[]{:S(2)}) %copy-start) | copy-done | bytes 114712
  2.2 0.0 copy-start.1
  2.2 0.8 %copy-done.1 = f32[3,4096]{1,0:T(4,128)S(1)} copy-done((f32[3,4096]{1,0:T(4,128)S(1)}, f32[3,4096]{1,0:T(4,128)}, u32[]{:S(2)}) %copy-start.1) | copy-done | bytes 49176
  3.1 0.0 copy-start.2
  3.1 0.7 copy-done.2
  3.8 0.0 copy-start.3
  3.8 0.7 copy-done.3
  4.5 28.5 %shard_map.64 = (f32[3,32,16,128]{3,2,1,0:T(8,128)S(1)}, f32[8,3,1024]{2,1,0:T(4,128)S(1)}, s32[8,1,128]{2,1,0:T(1,128)S(1)}) custom-call(f32[3,4096]{1,0:T(4,128)S(1)} %copy-done.1, f32[7,4096]{1,0:T(8,128)S(1)} %copy-done, s32[32,128]{1,0:T(8,128)S(1)} %bitcast.1, f32[3,1024]{1,0:T(4,128)S(1)} %copy-done.3, s32[1,8]{1,0:T(1,128)S(1)} %copy-done.4, ...), custom_call_target="tpu_custom_call" | custom-call | tf_op jit(solution)/shard_map/pallas_call | solution.py:178
  33.0 40.2 %shard_map.65.part = f32[8,8,1024]{2,1,0:T(8,128)S(1)} custom-call(s32[8,1,128]{2,1,0:T(1,128)S(1)} %get-tuple-element.8.lists, f32[3,32,16,128]{3,2,1,0:T(8,128)S(1)} %get-tuple-element.9.win, f32[8,3,1024]{2,1,0:T(4,128)S(1)} %get-tuple-element.10.vols), custom_call_target="tpu_custom_call" | custom-call | tf_op jit(solution)/shard_map/pallas_call | solution.py:274
  73.3 9.8 %shard_map.66 = f32[7,1024]{1,0:T(8,128)S(1)} custom-call(f32[8,8,1024]{2,1,0:T(8,128)S(1)} %shard_map.65.part), custom_call_target="tpu_custom_call" | custom-call | tf_op jit(solution)/shard_map/pallas_call | solution.py:317
  83.1 0.6 copy.9
Async XLA Ops:
  0.7 0.7 copy-start.4
  1.3 0.9 %copy-start = (f32[7,4096]{1,0:T(8,128)S(1)}, f32[7,4096]{1,0:T(8,128)}, u32[]{:S(2)}) copy-start(f32[7,4096]{1,0:T(8,128)} %mot.1) | copy-start | bytes 344068
  2.2 0.8 %copy-start.1 = (f32[3,4096]{1,0:T(4,128)S(1)}, f32[3,4096]{1,0:T(4,128)}, u32[]{:S(2)}) copy-start(f32[3,4096]{1,0:T(4,128)} %pos.1) | copy-start | bytes 147460
  3.1 0.7 copy-start.2
  3.8 0.7 copy-start.3

commit v2 on v1

v2 whole, which is shorter than its diff:
```python
import functools

import jax
import jax.numpy as jnp
from jax import lax
from jax.experimental import pallas as pl
from jax.experimental.pallas import tpu as pltpu
from jax.sharding import PartitionSpec as P

F32, BF16 = jnp.float32, jnp.bfloat16
MESH = pl.DeviceIdType.MESH
VMEM = pl.BlockSpec(memory_space=pltpu.VMEM)
SMEM = pl.BlockSpec(memory_space=pltpu.SMEM)
HBM = pl.BlockSpec(memory_space=pltpu.HBM)
ROWS = 10
LANES = 128
CORES = 2
DEPTH = 48


def dot(a, b, dims=((1,), (0,))):
    return lax.dot_general(a, b, (dims, ((), ())), preferred_element_type=F32)


def split3(x):
    first = x.astype(BF16).astype(F32)
    rest = x - first
    second = rest.astype(BF16).astype(F32)
    return first, second, (rest - second).astype(BF16).astype(F32)


def place():
    slab = lax.axis_index("slab")
    return slab // CORES, slab % CORES, lax.axis_index("grp")


def peer_of(me, offset, ngrp):
    other = (me + offset) % (CORES * ngrp)
    return other // ngrp, other % ngrp


def exchange_kernel(nchip, ngrp, pos_in, mot_in, bins_in, vol_in, infl, cnt, fs, mt, fv, lists,
                    pos, mot, bins, vols, xp, dcol, send, win,
                    in_sem, a_send, a_recv, f_send, f_recv, v_send, v_recv, l_send, l_recv):
    q, c, x = place()
    nz = nchip // ngrp
    blocks = bins.shape[0]
    nslab = nchip * CORES
    span = LANES // CORES
    members = CORES * ngrp
    me = c * ngrp + x
    up, down = (q + 1) % nchip, (q + nchip - 1) % nchip

    loads = [pltpu.make_async_copy(bins_in, bins, in_sem.at[0]), pltpu.make_async_copy(mot_in, mot, in_sem.at[1]),
             pltpu.make_async_copy(pos_in, pos, in_sem.at[2]), pltpu.make_async_copy(vol_in, vols.at[me], in_sem.at[3])]
    for load in loads:
        load.start()

    barrier = pltpu.get_barrier_semaphore()

    def greet(device):
        pl.semaphore_signal(barrier, inc=1, device_id=device, device_id_type=MESH)

    def greet_source(i, carry):
        greet((i * CORES + 1 - c, (x + ngrp - i // nz) % ngrp))
        return carry

    lax.fori_loop(0, nchip, greet_source, 0)
    greet((up * CORES + c, x))
    greet((down * CORES + c, x))
    for o in range(1, members):
        pc, px = peer_of(me, o, ngrp)
        greet((q * CORES + pc, px))

    lane = lax.broadcasted_iota(jnp.int32, (1, LANES), 1)
    row = jnp.where(lane == infl.shape[1], cnt[0], 0)
    for l in range(infl.shape[1]):
        row = jnp.where(lane == l, infl[0, l], row)
    lists[pl.ds(me, 1)] = row[None]

    loads[0].wait()
    slab_of = bins[...] // ngrp
    sub = lax.broadcasted_iota(jnp.int32, (nslab, LANES), 0)
    tri_r = lax.broadcasted_iota(jnp.int32, (LANES, 2 * LANES), 0)
    tri_c = lax.broadcasted_iota(jnp.int32, (LANES, 2 * LANES), 1)
    tri = jnp.where((tri_r <= tri_c), 1.0, 0.0).astype(BF16)
    carry = jnp.zeros((nslab, LANES), F32)
    for k in range(blocks):
        trow = slab_of[k : k + 1, :]
        hit = trow == sub
        cum = dot(jnp.where(hit, 1.0, 0.0).astype(BF16), tri)
        rank = jnp.sum(jnp.where(hit, cum[:, :LANES] + carry, 0.0), axis=0, keepdims=True)
        carry = carry + cum[:, LANES:]
        dest = trow.astype(F32) * span + (rank - 1.0)
        wide = jnp.broadcast_to(dest, (LANES, LANES)).T
        dcol[k * LANES : (k + 1) * LANES, :] = wide.astype(jnp.int32)

    for load in loads[1:]:
        load.wait()
    whole = jnp.concatenate([mot[...], pos[...], jnp.zeros((16 - ROWS, mot.shape[1]), F32)], axis=0)
    xp[...] = jnp.concatenate(split3(whole), axis=0).astype(BF16)

    slot = x * nz + q % nz
    wide2 = 2 * LANES
    steps = nchip // 4
    lane2 = lax.broadcasted_iota(jnp.int32, (wide2, LANES), 1)

    def to_bin(i):
        return pltpu.make_async_remote_copy(
            src_ref=send.at[i], dst_ref=win.at[1, slot], send_sem=a_send.at[i], recv_sem=a_recv.at[slot],
            device_id=(i * CORES + 1 - c, (x + q // nz) % ngrp), device_id_type=MESH)

    def send_four(i):
        first = (q // 4 + i) % steps * 4
        for k in range(4):
            to_bin(first + k).start()

    def group_of(j):
        o = (j + 1 - q // 4 % 2) % ngrp
        return (x + o + ngrp - q // nz) % ngrp

    def forward(j, to):
        part = pl.ds(group_of(j) * nz, nz)
        return pltpu.make_async_remote_copy(
            src_ref=win.at[1, part], dst_ref=win.at[0 if to == 0 else 2, part],
            send_sem=f_send.at[to, j], recv_sem=f_recv.at[to, group_of(j)],
            device_id=((up if to == 0 else down) * CORES + c, x), device_id_type=MESH)

    def forward_group(j):
        def arrived(z, _):
            s = group_of(j) * nz + z
            pltpu.make_async_remote_copy(
                src_ref=send.at[0], dst_ref=win.at[1, s], send_sem=a_send.at[0], recv_sem=a_recv.at[s],
                device_id=(q * CORES + 1 - c, x), device_id_type=MESH).wait_recv()
            return 0

        lax.fori_loop(0, nz, arrived, 0)
        forward(j, 0).start()
        forward(j, 1).start()

    def order(i, _):
        for half in range(2):
            tile = (q // 4 + i) % steps * 2 + half
            acc = jnp.zeros((48, wide2), F32)
            for k in range(blocks // 2):
                cols = slice(k * wide2, (k + 1) * wide2)
                d = dcol[cols, :] - tile * wide2
                one = jnp.concatenate(
                    [jnp.where(d == lane2, 1.0, 0.0), jnp.where(d == lane2 + LANES, 1.0, 0.0)], axis=1).astype(BF16)
                acc = acc + dot(xp[:, cols], one)
            full = acc[:16] + acc[16:32] + acc[32:]
            send[2 * tile] = full[:ROWS, :LANES]
            send[2 * tile + 1] = full[:ROWS, LANES:]

        @pl.when(i == 1)
        def _():
            pl.semaphore_wait(barrier, nchip + 2 + members - 1)
            send_four(0)
            for o in range(1, members):
                pc, px = peer_of(me, o, ngrp)
                for ref, s_sem, r_sem in ((vols, v_send, v_recv), (lists, l_send, l_recv)):
                    pltpu.make_async_remote_copy(
                        src_ref=ref.at[me], dst_ref=ref.at[me], send_sem=s_sem.at[o], recv_sem=r_sem.at[o],
                        device_id=(q * CORES + pc, px), device_id_type=MESH).start()

        @pl.when(i >= 1)
        def _():
            send_four(i)

        @pl.when(i == 4)
        def _():
            forward_group(0)

        @pl.when(i == 6)
        def _():
            forward_group(1)

        return 0

    lax.fori_loop(0, steps, order, 0)
    for j in range(2, ngrp):
        forward_group(j)

    left = lax.broadcasted_iota(jnp.int32, (ROWS, LANES), 1) < span
    row8 = lax.broadcasted_iota(jnp.int32, (8, LANES), 0)

    def prepare(chip, g):
        for k in range(nz // 2):
            a = win[chip, g * nz + 2 * k]
            b = win[chip, g * nz + 2 * k + 1]
            pair = (jnp.where(left, a, pltpu.roll(b, span, 1)), jnp.where(left, pltpu.roll(a, span, 1), b))
            cols = slice(k * LANES, (k + 1) * LANES)
            for tt in range(CORES):
                n = (chip * CORES + tt) * ngrp + g
                upper = pair[tt][:8]
                lower = jnp.concatenate([pair[tt][8:], jnp.zeros((16 - ROWS, LANES), F32)], axis=0)
                m1, m2, _ = split3(jnp.where(row8 == 7, 1.0, upper))
                mt[n, :, cols] = jnp.concatenate([m1, m2], axis=0).astype(BF16)
                x2, yz2 = upper * upper, lower * lower
                norm = x2[7:8] + yz2[0:1] + yz2[1:2] + 0.01
                y = -2.0 * jnp.where(row8 == 7, upper, lower)
                y = jnp.where(row8 == 2, norm, jnp.where(row8 == 3, 1.0, y))
                y1, y2, y3 = split3(y)
                fs[n, :, cols] = jnp.concatenate([y1, y2, y3, y1, y2, y1], axis=0).astype(BF16)

    def prepare_own(g, _):
        prepare(1, g)
        return 0

    lax.fori_loop(0, ngrp, prepare_own, 0)

    def vol_copies(o):
        other = (me + members - o) % members
        pc, px = peer_of(me, o, ngrp)
        return [pltpu.make_async_remote_copy(
            src_ref=ref.at[me], dst_ref=ref.at[other], send_sem=s_sem.at[o], recv_sem=r_sem.at[o],
            device_id=(q * CORES + pc, px), device_id_type=MESH)
            for ref, s_sem, r_sem in ((vols, v_send, v_recv), (lists, l_send, l_recv))]

    for o in range(1, members):
        for copy in vol_copies(o):
            copy.wait_recv()

    def prepare_vol(j, _):
        v = vols[j]
        v2 = v * v
        norm = v2[0:1] + v2[1:2] + v2[2:3]
        ones = jnp.ones_like(norm)
        zero = jnp.zeros_like(norm)
        w1, w2, w3 = split3(jnp.concatenate([v[1:3], ones, norm, zero, zero, zero, v[0:1]], axis=0))
        fv[j] = jnp.concatenate([w1, w1, w1, w2, w2, w3], axis=0).astype(BF16)
        return 0

    lax.fori_loop(0, members, prepare_vol, 0)

    def arrived_near(j, _):
        for to in range(2):
            part = pl.ds(j * nz, nz)
            pltpu.make_async_remote_copy(
                src_ref=win.at[1, part], dst_ref=win.at[0 if to == 0 else 2, part],
                send_sem=f_send.at[to, 0], recv_sem=f_recv.at[to, j],
                device_id=((up if to == 0 else down) * CORES + c, x), device_id_type=MESH).wait_recv()
        prepare(0, j)
        prepare(2, j)
        return 0

    lax.fori_loop(0, ngrp, arrived_near, 0)

    def sent(i, _):
        to_bin(i).wait_send()
        return 0

    lax.fori_loop(0, nchip, sent, 0)
    for o in range(1, members):
        for copy in vol_copies(o):
            copy.wait_send()
    for j in range(ngrp):
        for to in range(2):
            forward(j, to).wait_send()


def exchange(nchip, ngrp, pos, mot, bins, vol, infl, cnt):
    members = CORES * ngrp
    nvol = vol.shape[1]
    width = pos.shape[1]
    nbin = 3 * CORES * ngrp
    nodes = nchip // ngrp * LANES // CORES
    dma = pltpu.SemaphoreType.DMA
    return pl.pallas_call(
        functools.partial(exchange_kernel, nchip, ngrp),
        out_shape=(
            jax.ShapeDtypeStruct((nbin, DEPTH, nodes), BF16),
            jax.ShapeDtypeStruct((nbin, 16, nodes), BF16),
            jax.ShapeDtypeStruct((members, DEPTH, nvol), BF16),
            jax.ShapeDtypeStruct((members, 1, LANES), jnp.int32),
        ),
        in_specs=[HBM, HBM, HBM, HBM, SMEM, SMEM],
        out_specs=(VMEM, VMEM, VMEM, VMEM),
        scratch_shapes=[
            pltpu.VMEM(pos.shape, F32),
            pltpu.VMEM(mot.shape, F32),
            pltpu.VMEM(bins.shape, jnp.int32),
            pltpu.VMEM((members, 3, nvol), F32),
            pltpu.VMEM((48, width), BF16),
            pltpu.VMEM((width, LANES), jnp.int32),
            pltpu.VMEM((nchip, ROWS, LANES), F32),
            pltpu.VMEM((3, nchip, ROWS, LANES), F32),
            dma((4,)),
            dma((nchip,)), dma((nchip,)),
            dma((2, ngrp)), dma((2, ngrp)),
            dma((members,)), dma((members,)),
            dma((members,)), dma((members,)),
        ],
        compiler_params=pltpu.CompilerParams(collective_id=0, has_side_effects=True, vmem_limit_bytes=40 << 20),
    )(pos, mot, bins, vol, infl, cnt)


def blend_kernel(ngrp, lmax, lists, fs, mt, fv, part, acc, block_of, bin_of):
    q, _, _ = place()
    members = fv.shape[0]
    base = (q - 1) * CORES * ngrp

    def block(j, filled):
        acc[j] = jnp.zeros(acc.shape[1:], F32)

        def entry(l, filled):
            block_of[filled] = j
            bin_of[filled] = lists[j, 0, l] - base
            return filled + 1

        return lax.fori_loop(0, lists[j, 0, lmax], entry, filled)

    total = lax.fori_loop(0, members, block, 0)

    def together(first, many):
        js = [block_of[first + k] for k in range(many)]
        ns = [bin_of[first + k] for k in range(many)]
        r2 = [dot(fs[n], fv[j], ((0,), (0,))) for j, n in zip(js, ns)]
        for j, n, d in zip(js, ns, r2):
            w = pltpu.reciprocal(d * d, approx=True)
            w1 = w.astype(BF16)
            w2 = (w - w1.astype(F32)).astype(BF16)
            m = mt[n]
            acc[j] += dot(m, w1) + dot(m, w2)

    def four(i, _):
        together(4 * i, 4)
        return 0

    def one(i, _):
        together(i, 1)
        return 0

    lax.fori_loop(0, total // 4, four, 0)
    lax.fori_loop(total // 4 * 4, total, one, 0)

    def close(j, _):
        part[j] = acc[j, :8] + acc[j, 8:]
        return 0

    lax.fori_loop(0, members, close, 0)


def blend(ngrp, lmax, lists, fs, mt, fv):
    members, _, nvol = fv.shape
    return pl.pallas_call(
        functools.partial(blend_kernel, ngrp, lmax),
        out_shape=jax.ShapeDtypeStruct((members, 8, nvol), F32),
        in_specs=[SMEM, VMEM, VMEM, VMEM],
        out_specs=VMEM,
        scratch_shapes=[
            pltpu.VMEM((members, 16, nvol), F32),
            pltpu.SMEM((members * lmax,), jnp.int32),
            pltpu.SMEM((members * lmax,), jnp.int32),
        ],
        compiler_params=pltpu.CompilerParams(vmem_limit_bytes=48 << 20),
    )(lists, fs, mt, fv)


def combine_kernel(ngrp, part, out, got, s_sem, r_sem):
    q, c, x = place()
    members = CORES * ngrp
    me = c * ngrp + x
    barrier = pltpu.get_barrier_semaphore()
    for o in range(1, members):
        pc, px = peer_of(me, o, ngrp)
        pl.semaphore_signal(barrier, inc=1, device_id=(q * CORES + pc, px), device_id_type=MESH)
    pl.semaphore_wait(barrier, members - 1)
    copies = []
    for o in range(1, members):
        pc, px = peer_of(me, o, ngrp)
        copy = pltpu.make_async_remote_copy(
            src_ref=part.at[(me + o) % members], dst_ref=got.at[o], send_sem=s_sem.at[o], recv_sem=r_sem.at[o],
            device_id=(q * CORES + pc, px), device_id_type=MESH)
        copy.start()
        copies.append(copy)
    total = part[me]
    for o in range(1, members):
        copies[o - 1].wait_recv()
        total = total + got[o]
    out[...] = total[:7] / total[7:8]
    for copy in copies:
        copy.wait_send()


def combine(ngrp, part):
    members, _, nvol = part.shape
    return pl.pallas_call(
        functools.partial(combine_kernel, ngrp),
        out_shape=jax.ShapeDtypeStruct((7, nvol), F32),
        in_specs=[VMEM],
        out_specs=VMEM,
        scratch_shapes=[
            pltpu.VMEM((members, 8, nvol), F32),
            pltpu.SemaphoreType.DMA((members,)),
            pltpu.SemaphoreType.DMA((members,)),
        ],
        compiler_params=pltpu.CompilerParams(collective_id=1, has_side_effects=True, vmem_limit_bytes=48 << 20),
    )(part)


def on_device(surf_pos, surf_motion, surf_bin, vol_pos, influence, list_count):
    nchip = lax.axis_size("slab") // CORES
    ngrp = lax.axis_size("grp")
    bins = surf_bin.reshape(-1, LANES)
    fs, mt, fv, lists = exchange(nchip, ngrp, surf_pos, surf_motion, bins, vol_pos, influence, list_count)
    part = blend(ngrp, influence.shape[1], lists, fs, mt, fv)
    return combine(ngrp, part)


def solution(mesh):
    return jax.shard_map(
        on_device,
        mesh=mesh,
        in_specs=(
            P(None, ("slab", "grp")),
            P(None, ("slab", "grp")),
            P(("slab", "grp")),
            P(None, ("slab", "grp")),
            P(("slab", "grp"), None),
            P(("slab", "grp")),
        ),
        out_specs=P(None, ("slab", "grp")),
        check_vma=False,
    )
```

time: 84 us -> 74.7 us (0.89)
  the two profiles are of different devices: /device:TPU:56 before, /device:TPU:104 now
where the time goes in v2:
time: 74.7 us; the launch traced here: 74.4 us
  Pallas kernels  69.3 us (93%)
  local copies, waits for them, and re-layouts  4.44 us (6%)
    pallas_call x1, Pallas kernels, blend(): pl.pallas_call(functools.partial(blend_kernel, ngrp, lmax), out_shape=jax...  33.4 us
    pallas_call x1, Pallas kernels, exchange(): pl.pallas_call(functools.partial(exchange_kernel, nchip, ngrp), out_shape...  28.1 us
    pallas_call x1, Pallas kernels, combine(): pl.pallas_call(functools.partial(combine_kernel, ngrp), out_shape=jax.Sha...  7.73 us
    unnamed x11, local copies, waits for them, and re-layouts  4.44 us

profile of v2, /device:TPU:104, one launch (start us, length us, event | category | flops | bytes accessed | tf_op | source)
XLA Modules:
  0.0 74.4 jit_solution(266313447705468177)
XLA Ops:
  0.7 0.0 copy-start
  0.7 0.9 %copy-done = f32[7,4096]{1,0:T(8,128)S(1)} copy-done((f32[7,4096]{1,0:T(8,128)S(1)}, f32[7,4096]{1,0:T(8,128)}, u32[]{:S(2)}) %copy-start) | copy-done | bytes 114712
  1.6 0.0 copy-start.1
  1.6 0.8 %copy-done.1 = f32[3,4096]{1,0:T(4,128)S(1)} copy-done((f32[3,4096]{1,0:T(4,128)S(1)}, f32[3,4096]{1,0:T(4,128)}, u32[]{:S(2)}) %copy-start.1) | copy-done | bytes 49176
  2.4 0.0 copy-start.2
  2.4 0.7 copy-done.2
  3.1 0.0 copy-start.3
  3.1 0.7 copy-done.3
  3.8 0.0 copy-start.4
  3.8 0.7 copy-done.4
  4.5 28.1 %shard_map.64 = (bf16[24,48,512]{2,1,0:T(8,128)(2,1)S(1)}, bf16[24,16,512]{2,1,0:T(8,128)(2,1)S(1)}, bf16[8,48,1024]{2,1,0:T(8,128)(2,1)S(1)}, s32[8,1,128]{2,1,0:T(1,128)S(1)}) custom-call(f32[3,4096]{1,0:T(4,128)S(1)} %copy-done.1, f32[7,4096]{1,0:T(8,128)S(1)} %copy-done, s32[32,128]{1,0:T(8,128)S(1)} %bitcast.1, f32[3,1024]{1,0:T(4,128)S(1)} %copy-done.3, ...), custom_call_target="tpu_custom_call" | custom-call | tf_op jit(solution)/shard_map/pallas_call | solution.py:269
  32.6 33.4 %shard_map.65.part = f32[8,8,1024]{2,1,0:T(8,128)S(1)} custom-call(s32[8,1,128]{2,1,0:T(1,128)S(1)} %get-tuple-element.9.lists, bf16[24,48,512]{2,1,0:T(8,128)(2,1)S(1)} %get-tuple-element.10.fs, bf16[24,16,512]{2,1,0:T(8,128)(2,1)S(1)} %get-tuple-element.11.mt, bf16[8,48,1024]{2,1,0:T(8,128)(2,1)S(1)} %get-tuple-element.12.fv), custom_call_target="tpu_custom_call" | custom-call | tf_op jit(solution)/shard_map/pallas_call | solution.py:346
  66.0 7.7 %shard_map.66 = f32[7,1024]{1,0:T(8,128)S(1)} custom-call(f32[8,8,1024]{2,1,0:T(8,128)S(1)} %shard_map.65.part), custom_call_target="tpu_custom_call" | custom-call | tf_op jit(solution)/shard_map/pallas_call | solution.py:388
  73.8 0.6 copy.9
Async XLA Ops:
  0.7 0.9 %copy-start = (f32[7,4096]{1,0:T(8,128)S(1)}, f32[7,4096]{1,0:T(8,128)}, u32[]{:S(2)}) copy-start(f32[7,4096]{1,0:T(8,128)} %mot_in.1) | copy-start | bytes 344068
  1.6 0.8 %copy-start.1 = (f32[3,4096]{1,0:T(4,128)S(1)}, f32[3,4096]{1,0:T(4,128)}, u32[]{:S(2)}) copy-start(f32[3,4096]{1,0:T(4,128)} %pos_in.1) | copy-start | bytes 147460
  2.4 0.7 copy-start.2
  3.1 0.7 copy-start.3
  3.8 0.7 copy-start.4

commit v3 on v2

--- a/solution.py
+++ b/solution.py
@@ -15,6 +15,7 @@
 ROWS = 10
 LANES = 128
 CORES = 2
+EARLY = 4
 DEPTH = 48
 
 
@@ -39,8 +40,8 @@
     return other // ngrp, other % ngrp
 
 
-def exchange_kernel(nchip, ngrp, pos_in, mot_in, bins_in, vol_in, infl, cnt, fs, mt, fv, lists,
-                    pos, mot, bins, vols, xp, dcol, send, win,
+def exchange_kernel(nchip, ngrp, pos_in, mot_in, bins_in, vol_in, infl_in, cnt, fs, mt, fv, lists,
+                    infl, pos, mot, bins, vols, xp, dcol, send, win,
                     in_sem, a_send, a_recv, f_send, f_recv, v_send, v_recv, l_send, l_recv):
     q, c, x = place()
     nz = nchip // ngrp
@@ -51,8 +52,24 @@
     me = c * ngrp + x
     up, down = (q + 1) % nchip, (q + nchip - 1) % nchip
 
+    y, z, ny = q // nz, q % nz, nchip // nz
+
+    def shift(i):
+        j = i // nz
+        return j + j // 2 * (1 - 2 * (j % 2))
+
+    def chip_at(i, sign):
+        kz, ky = i // ny, i % ny
+        dz = nz // 2 + (kz + 1) // 2 * (1 - 2 * (kz % 2))
+        dy = ny // 2 + (ky + 1) // 2 * (1 - 2 * (ky % 2))
+        return (y + ny + sign * dy) % ny * nz + (z + nz + sign * dz) % nz
+
+    def met(i, sign):
+        return chip_at(i, sign) * CORES + c, (x + ngrp + sign * shift(i)) % ngrp
+
     loads = [pltpu.make_async_copy(bins_in, bins, in_sem.at[0]), pltpu.make_async_copy(mot_in, mot, in_sem.at[1]),
-             pltpu.make_async_copy(pos_in, pos, in_sem.at[2]), pltpu.make_async_copy(vol_in, vols.at[me], in_sem.at[3])]
+             pltpu.make_async_copy(pos_in, pos, in_sem.at[2]), pltpu.make_async_copy(vol_in, vols.at[me], in_sem.at[3]),
+             pltpu.make_async_copy(infl_in, infl, in_sem.at[4])]
     for load in loads:
         load.start()
 
@@ -62,7 +79,7 @@
         pl.semaphore_signal(barrier, inc=1, device_id=device, device_id_type=MESH)
 
     def greet_source(i, carry):
-        greet((i * CORES + 1 - c, (x + ngrp - i // nz) % ngrp))
+        greet(met(i, -1))
         return carry
 
     lax.fori_loop(0, nchip, greet_source, 0)
@@ -71,12 +88,6 @@
     for o in range(1, members):
         pc, px = peer_of(me, o, ngrp)
         greet((q * CORES + pc, px))
-
-    lane = lax.broadcasted_iota(jnp.int32, (1, LANES), 1)
-    row = jnp.where(lane == infl.shape[1], cnt[0], 0)
-    for l in range(infl.shape[1]):
-        row = jnp.where(lane == l, infl[0, l], row)
-    lists[pl.ds(me, 1)] = row[None]
 
     loads[0].wait()
     slab_of = bins[...] // ngrp
@@ -97,65 +108,76 @@
 
     for load in loads[1:]:
         load.wait()
+    lane = lax.broadcasted_iota(jnp.int32, (1, LANES), 1)
+    row = jnp.where(lane == infl.shape[1], cnt[0], 0)
+    for l in range(infl.shape[1]):
+        row = jnp.where(lane == l, infl[0, l], row)
+    lists[pl.ds(me, 1)] = row[None]
+
     whole = jnp.concatenate([mot[...], pos[...], jnp.zeros((16 - ROWS, mot.shape[1]), F32)], axis=0)
     xp[...] = jnp.concatenate(split3(whole), axis=0).astype(BF16)
 
-    slot = x * nz + q % nz
-    wide2 = 2 * LANES
     steps = nchip // 4
-    lane2 = lax.broadcasted_iota(jnp.int32, (wide2, LANES), 1)
+    lanes = lax.broadcasted_iota(jnp.int32, (1, LANES), 1)
 
     def to_bin(i):
+        slot = x * nz + i % nz
         return pltpu.make_async_remote_copy(
             src_ref=send.at[i], dst_ref=win.at[1, slot], send_sem=a_send.at[i], recv_sem=a_recv.at[slot],
-            device_id=(i * CORES + 1 - c, (x + q // nz) % ngrp), device_id_type=MESH)
-
-    def send_four(i):
-        first = (q // 4 + i) % steps * 4
-        for k in range(4):
-            to_bin(first + k).start()
+            device_id=met(i, 1), device_id_type=MESH)
+
+    def send_one(i, _):
+        to_bin(i).start()
+        return 0
 
     def group_of(j):
-        o = (j + 1 - q // 4 % 2) % ngrp
-        return (x + o + ngrp - q // nz) % ngrp
+        return (x + ngrp - shift(j * nz)) % ngrp
 
     def forward(j, to):
         part = pl.ds(group_of(j) * nz, nz)
         return pltpu.make_async_remote_copy(
             src_ref=win.at[1, part], dst_ref=win.at[0 if to == 0 else 2, part],
-            send_sem=f_send.at[to, j], recv_sem=f_recv.at[to, group_of(j)],
+            send_sem=f_send.at[to, j], recv_sem=f_recv.at[to, j],
             device_id=((up if to == 0 else down) * CORES + c, x), device_id_type=MESH)
 
-    def forward_group(j):
-        def arrived(z, _):
-            s = group_of(j) * nz + z
+    def forward_group(j, _):
+        def arrived(k, _):
+            s = group_of(j) * nz + k
             pltpu.make_async_remote_copy(
                 src_ref=send.at[0], dst_ref=win.at[1, s], send_sem=a_send.at[0], recv_sem=a_recv.at[s],
-                device_id=(q * CORES + 1 - c, x), device_id_type=MESH).wait_recv()
+                device_id=met(0, 1), device_id_type=MESH).wait_recv()
             return 0
 
         lax.fori_loop(0, nz, arrived, 0)
         forward(j, 0).start()
         forward(j, 1).start()
+        return 0
 
     def order(i, _):
         for half in range(2):
-            tile = (q // 4 + i) % steps * 2 + half
-            acc = jnp.zeros((48, wide2), F32)
+            r = 4 * i + 2 * half
+            want = [jnp.broadcast_to(lanes + chip_at(r + k, 1) * LANES, (2 * LANES, LANES)) for k in range(2)]
+            acc = jnp.zeros((48, 2 * LANES), F32)
             for k in range(blocks // 2):
-                cols = slice(k * wide2, (k + 1) * wide2)
-                d = dcol[cols, :] - tile * wide2
-                one = jnp.concatenate(
-                    [jnp.where(d == lane2, 1.0, 0.0), jnp.where(d == lane2 + LANES, 1.0, 0.0)], axis=1).astype(BF16)
+                cols = slice(k * 2 * LANES, (k + 1) * 2 * LANES)
+                d = dcol[cols, :]
+                one = jnp.concatenate([jnp.where(d == w, 1.0, 0.0) for w in want], axis=1).astype(BF16)
                 acc = acc + dot(xp[:, cols], one)
             full = acc[:16] + acc[16:32] + acc[32:]
-            send[2 * tile] = full[:ROWS, :LANES]
-            send[2 * tile + 1] = full[:ROWS, LANES:]
-
-        @pl.when(i == 1)
+            send[r] = full[:ROWS, :LANES]
+            send[r + 1] = full[:ROWS, LANES:]
+
+        @pl.when(i == EARLY)
         def _():
             pl.semaphore_wait(barrier, nchip + 2 + members - 1)
-            send_four(0)
+            lax.fori_loop(0, 4 * EARLY, send_one, 0)
+
+        @pl.when(i >= EARLY)
+        def _():
+            lax.fori_loop(4 * i, 4 * i + 4, send_one, 0)
+
+        @pl.when(i == EARLY)
+        def _():
             for o in range(1, members):
                 pc, px = peer_of(me, o, ngrp)
                 for ref, s_sem, r_sem in ((vols, v_send, v_recv), (lists, l_send, l_recv)):
@@ -163,23 +185,10 @@
                         src_ref=ref.at[me], dst_ref=ref.at[me], send_sem=s_sem.at[o], recv_sem=r_sem.at[o],
                         device_id=(q * CORES + pc, px), device_id_type=MESH).start()
 
-        @pl.when(i >= 1)
-        def _():
-            send_four(i)
-
-        @pl.when(i == 4)
-        def _():
-            forward_group(0)
-
-        @pl.when(i == 6)
-        def _():
-            forward_group(1)
-
         return 0
 
     lax.fori_loop(0, steps, order, 0)
-    for j in range(2, ngrp):
-        forward_group(j)
+    lax.fori_loop(0, ngrp, forward_group, 0)
 
     left = lax.broadcasted_iota(jnp.int32, (ROWS, LANES), 1) < span
     row8 = lax.broadcasted_iota(jnp.int32, (8, LANES), 0)
@@ -235,13 +244,9 @@
 
     def arrived_near(j, _):
         for to in range(2):
-            part = pl.ds(j * nz, nz)
-            pltpu.make_async_remote_copy(
-                src_ref=win.at[1, part], dst_ref=win.at[0 if to == 0 else 2, part],
-                send_sem=f_send.at[to, 0], recv_sem=f_recv.at[to, j],
-                device_id=((up if to == 0 else down) * CORES + c, x), device_id_type=MESH).wait_recv()
-        prepare(0, j)
-        prepare(2, j)
+            forward(j, to).wait_recv()
+        prepare(0, group_of(j))
+        prepare(2, group_of(j))
         return 0
 
     lax.fori_loop(0, ngrp, arrived_near, 0)
@@ -274,9 +279,10 @@
             jax.ShapeDtypeStruct((members, DEPTH, nvol), BF16),
             jax.ShapeDtypeStruct((members, 1, LANES), jnp.int32),
         ),
-        in_specs=[HBM, HBM, HBM, HBM, SMEM, SMEM],
+        in_specs=[HBM] * 5 + [SMEM],
         out_specs=(VMEM, VMEM, VMEM, VMEM),
         scratch_shapes=[
+            pltpu.SMEM(infl.shape, jnp.int32),
             pltpu.VMEM(pos.shape, F32),
             pltpu.VMEM(mot.shape, F32),
             pltpu.VMEM(bins.shape, jnp.int32),
@@ -285,7 +291,7 @@
             pltpu.VMEM((width, LANES), jnp.int32),
             pltpu.VMEM((nchip, ROWS, LANES), F32),
             pltpu.VMEM((3, nchip, ROWS, LANES), F32),
-            dma((4,)),
+            dma((5,)),
             dma((nchip,)), dma((nchip,)),
             dma((2, ngrp)), dma((2, ngrp)),
             dma((members,)), dma((members,)),
@@ -403,6 +409,8 @@
     nchip = lax.axis_size("slab") // CORES
     ngrp = lax.axis_size("grp")
     bins = surf_bin.reshape(-1, LANES)
+    surf_pos, surf_motion, bins, vol_pos, influence = (
+        pltpu.with_memory_space_constraint(a, pltpu.HBM) for a in (surf_pos, surf_motion, bins, vol_pos, influence))
     fs, mt, fv, lists = exchange(nchip, ngrp, surf_pos, surf_motion, bins, vol_pos, influence, list_count)
     part = blend(ngrp, influence.shape[1], lists, fs, mt, fv)
     return combine(ngrp, part)

time: 74.7 us -> 72.2 us (0.967)
  the two profiles are of different devices: /device:TPU:104 before, /device:TPU:8 now
where the time goes in v3:
time: 72.2 us; the launch traced here: 72.1 us
  Pallas kernels  70.9 us (98%)
    pallas_call x1, Pallas kernels, blend(): pl.pallas_call(functools.partial(blend_kernel, ngrp, lmax), out_shape=jax...  35 us
    pallas_call x1, Pallas kernels, exchange(): pl.pallas_call(functools.partial(exchange_kernel, nchip, ngrp), out_shape...  28.1 us
    pallas_call x1, Pallas kernels, combine(): pl.pallas_call(functools.partial(combine_kernel, ngrp), out_shape=jax.Sha...  7.73 us

profile of v3, /device:TPU:8, one launch (start us, length us, event | category | flops | bytes accessed | tf_op | source)
XLA Modules:
  0.0 72.1 jit_solution(9228348962898052889)
XLA Ops:
  0.7 28.1 %shard_map.64 = (bf16[24,48,512]{2,1,0:T(8,128)(2,1)S(1)}, bf16[24,16,512]{2,1,0:T(8,128)(2,1)S(1)}, bf16[8,48,1024]{2,1,0:T(8,128)(2,1)S(1)}, s32[8,1,128]{2,1,0:T(1,128)S(1)}) custom-call(f32[3,4096]{1,0:T(4,128)} %pos_in.1, f32[7,4096]{1,0:T(8,128)} %mot_in.1, s32[32,128]{1,0:T(8,128)} %bitcast.1, f32[3,1024]{1,0:T(4,128)} %vol_in.1, s32[1,8]{1,0:T(1,128)} %infl_in.1, ...), custom_call_target="tpu_custom_call" | custom-call | tf_op jit(solution)/shard_map/pallas_call | solution.py:274
  28.8 35.0 %shard_map.65.part = f32[8,8,1024]{2,1,0:T(8,128)S(1)} custom-call(s32[8,1,128]{2,1,0:T(1,128)S(1)} %get-tuple-element.9.lists, bf16[24,48,512]{2,1,0:T(8,128)(2,1)S(1)} %get-tuple-element.10.fs, bf16[24,16,512]{2,1,0:T(8,128)(2,1)S(1)} %get-tuple-element.11.mt, bf16[8,48,1024]{2,1,0:T(8,128)(2,1)S(1)} %get-tuple-element.12.fv), custom_call_target="tpu_custom_call" | custom-call | tf_op jit(solution)/shard_map/pallas_call | solution.py:352
  63.8 7.7 %shard_map.66 = f32[7,1024]{1,0:T(8,128)S(1)} custom-call(f32[8,8,1024]{2,1,0:T(8,128)S(1)} %shard_map.65.part), custom_call_target="tpu_custom_call" | custom-call | tf_op jit(solution)/shard_map/pallas_call | solution.py:394
  71.5 0.6 copy.9

commit v4 on v3

--- a/solution.py
+++ b/solution.py
@@ -15,7 +15,6 @@
 ROWS = 10
 LANES = 128
 CORES = 2
-EARLY = 4
 DEPTH = 48
 
 
@@ -41,7 +40,7 @@
 
 
 def exchange_kernel(nchip, ngrp, pos_in, mot_in, bins_in, vol_in, infl_in, cnt, fs, mt, fv, lists,
-                    infl, pos, mot, bins, vols, xp, dcol, send, win,
+                    infl, pos, mot, bins, vols, xp, one, acc, send, win,
                     in_sem, a_send, a_recv, f_send, f_recv, v_send, v_recv, l_send, l_recv):
     q, c, x = place()
     nz = nchip // ngrp
@@ -96,15 +95,18 @@
     tri_c = lax.broadcasted_iota(jnp.int32, (LANES, 2 * LANES), 1)
     tri = jnp.where((tri_r <= tri_c), 1.0, 0.0).astype(BF16)
     carry = jnp.zeros((nslab, LANES), F32)
+    fold = 2 * LANES // span
+    column = lax.broadcasted_iota(jnp.int32, (LANES, LANES), 1).astype(F32)
     for k in range(blocks):
         trow = slab_of[k : k + 1, :]
         hit = trow == sub
         cum = dot(jnp.where(hit, 1.0, 0.0).astype(BF16), tri)
         rank = jnp.sum(jnp.where(hit, cum[:, :LANES] + carry, 0.0), axis=0, keepdims=True)
         carry = carry + cum[:, LANES:]
-        dest = trow.astype(F32) * span + (rank - 1.0)
+        dest = (trow % fold * span).astype(F32) + (rank - 1.0)
         wide = jnp.broadcast_to(dest, (LANES, LANES)).T
-        dcol[k * LANES : (k + 1) * LANES, :] = wide.astype(jnp.int32)
+        one[k * LANES : (k + 1) * LANES, :] = jnp.concatenate(
+            [jnp.where(wide == column + h * LANES, 1.0, 0.0) for h in range(2)], axis=1).astype(BF16)
 
     for load in loads[1:]:
         load.wait()
@@ -115,15 +117,12 @@
     lists[pl.ds(me, 1)] = row[None]
 
     whole = jnp.concatenate([mot[...], pos[...], jnp.zeros((16 - ROWS, mot.shape[1]), F32)], axis=0)
-    xp[...] = jnp.concatenate(split3(whole), axis=0).astype(BF16)
-
-    steps = nchip // 4
-    lanes = lax.broadcasted_iota(jnp.int32, (1, LANES), 1)
+    xp[...] = jnp.concatenate(split3(whole), axis=0)
 
     def to_bin(i):
         slot = x * nz + i % nz
         return pltpu.make_async_remote_copy(
-            src_ref=send.at[i], dst_ref=win.at[1, slot], send_sem=a_send.at[i], recv_sem=a_recv.at[slot],
+            src_ref=send.at[chip_at(i, 1)], dst_ref=win.at[1, slot], send_sem=a_send.at[i], recv_sem=a_recv.at[slot],
             device_id=met(i, 1), device_id_type=MESH)
 
     def send_one(i, _):
@@ -153,41 +152,29 @@
         forward(j, 1).start()
         return 0
 
-    def order(i, _):
-        for half in range(2):
-            r = 4 * i + 2 * half
-            want = [jnp.broadcast_to(lanes + chip_at(r + k, 1) * LANES, (2 * LANES, LANES)) for k in range(2)]
-            acc = jnp.zeros((48, 2 * LANES), F32)
-            for k in range(blocks // 2):
-                cols = slice(k * 2 * LANES, (k + 1) * 2 * LANES)
-                d = dcol[cols, :]
-                one = jnp.concatenate([jnp.where(d == w, 1.0, 0.0) for w in want], axis=1).astype(BF16)
-                acc = acc + dot(xp[:, cols], one)
-            full = acc[:16] + acc[16:32] + acc[32:]
-            send[r] = full[:ROWS, :LANES]
-            send[r + 1] = full[:ROWS, LANES:]
-
-        @pl.when(i == EARLY)
-        def _():
-            pl.semaphore_wait(barrier, nchip + 2 + members - 1)
-            lax.fori_loop(0, 4 * EARLY, send_one, 0)
-
-        @pl.when(i >= EARLY)
-        def _():
-            lax.fori_loop(4 * i, 4 * i + 4, send_one, 0)
-
-        @pl.when(i == EARLY)
-        def _():
-            for o in range(1, members):
-                pc, px = peer_of(me, o, ngrp)
-                for ref, s_sem, r_sem in ((vols, v_send, v_recv), (lists, l_send, l_recv)):
-                    pltpu.make_async_remote_copy(
-                        src_ref=ref.at[me], dst_ref=ref.at[me], send_sem=s_sem.at[o], recv_sem=r_sem.at[o],
-                        device_id=(q * CORES + pc, px), device_id_type=MESH).start()
-
-        return 0
-
-    lax.fori_loop(0, steps, order, 0)
+    tiles = slab_of // fold
+    ntile = nslab // fold
+    rows = 4
+    for k in range(blocks // rows):
+        cols = slice(k * rows * LANES, (k + 1) * rows * LANES)
+        mine = jnp.concatenate([tiles[k * rows + r : k * rows + r + 1, :] for r in range(rows)], axis=1)
+        piece = xp[:, cols]
+        kept = jnp.concatenate([jnp.where(mine == p, piece, 0.0) for p in range(ntile)], axis=0).astype(BF16)
+        product = dot(kept, one[cols, :])
+        acc[...] = product if k == 0 else acc[...] + product
+    for p in range(ntile):
+        full = acc[48 * p : 48 * p + 16] + acc[48 * p + 16 : 48 * p + 32] + acc[48 * p + 32 : 48 * p + 48]
+        send[2 * p] = full[:ROWS, :LANES]
+        send[2 * p + 1] = full[:ROWS, LANES:]
+
+    pl.semaphore_wait(barrier, nchip + 2 + members - 1)
+    lax.fori_loop(0, nchip, send_one, 0)
+    for o in range(1, members):
+        pc, px = peer_of(me, o, ngrp)
+        for ref, s_sem, r_sem in ((vols, v_send, v_recv), (lists, l_send, l_recv)):
+            pltpu.make_async_remote_copy(
+                src_ref=ref.at[me], dst_ref=ref.at[me], send_sem=s_sem.at[o], recv_sem=r_sem.at[o],
+                device_id=(q * CORES + pc, px), device_id_type=MESH).start()
     lax.fori_loop(0, ngrp, forward_group, 0)
 
     left = lax.broadcasted_iota(jnp.int32, (ROWS, LANES), 1) < span
@@ -287,8 +274,9 @@
             pltpu.VMEM(mot.shape, F32),
             pltpu.VMEM(bins.shape, jnp.int32),
             pltpu.VMEM((members, 3, nvol), F32),
-            pltpu.VMEM((48, width), BF16),
-            pltpu.VMEM((width, LANES), jnp.int32),
+            pltpu.VMEM((48, width), F32),
+            pltpu.VMEM((width, 2 * LANES), BF16),
+            pltpu.VMEM((nchip // 2 * 48, 2 * LANES), F32),
             pltpu.VMEM((nchip, ROWS, LANES), F32),
             pltpu.VMEM((3, nchip, ROWS, LANES), F32),
             dma((5,)),
@@ -363,44 +351,52 @@
     )(lists, fs, mt, fv)
 
 
-def combine_kernel(ngrp, part, out, got, s_sem, r_sem):
+def combine_kernel(ngrp, part, out, across, along, sums, c_send, c_recv, x_send, x_recv):
     q, c, x = place()
-    members = CORES * ngrp
-    me = c * ngrp + x
     barrier = pltpu.get_barrier_semaphore()
-    for o in range(1, members):
-        pc, px = peer_of(me, o, ngrp)
-        pl.semaphore_signal(barrier, inc=1, device_id=(q * CORES + pc, px), device_id_type=MESH)
-    pl.semaphore_wait(barrier, members - 1)
-    copies = []
-    for o in range(1, members):
-        pc, px = peer_of(me, o, ngrp)
+    there = (q * CORES + 1 - c, x)
+    pl.semaphore_signal(barrier, inc=1, device_id=there, device_id_type=MESH)
+    for o in range(1, ngrp):
+        pl.semaphore_signal(barrier, inc=1, device_id=(q * CORES + c, (x + o) % ngrp), device_id_type=MESH)
+    pl.semaphore_wait(barrier, ngrp)
+
+    crossing = []
+    for o in (2, 1, 3, 0):
+        to = (x + o) % ngrp
         copy = pltpu.make_async_remote_copy(
-            src_ref=part.at[(me + o) % members], dst_ref=got.at[o], send_sem=s_sem.at[o], recv_sem=r_sem.at[o],
-            device_id=(q * CORES + pc, px), device_id_type=MESH)
+            src_ref=part.at[(1 - c) * ngrp + to], dst_ref=across.at[to], send_sem=c_send.at[to], recv_sem=c_recv.at[to],
+            device_id=there, device_id_type=MESH)
         copy.start()
-        copies.append(copy)
-    total = part[me]
-    for o in range(1, members):
-        copies[o - 1].wait_recv()
-        total = total + got[o]
+        crossing.append((o, to, copy))
+    moving = []
+    for o, to, copy in crossing[:-1]:
+        copy.wait_recv()
+        sums[o] = part[c * ngrp + to] + across[to]
+        step = pltpu.make_async_remote_copy(
+            src_ref=sums.at[o], dst_ref=along.at[o], send_sem=x_send.at[o], recv_sem=x_recv.at[o],
+            device_id=(q * CORES + c, to), device_id_type=MESH)
+        step.start()
+        moving.append((o, step))
+    crossing[-1][2].wait_recv()
+    total = part[c * ngrp + x] + across[x]
+    for o, step in moving:
+        step.wait_recv()
+        total = total + along[o]
     out[...] = total[:7] / total[7:8]
-    for copy in copies:
+    for _, _, copy in crossing:
         copy.wait_send()
+    for _, step in moving:
+        step.wait_send()
 
 
 def combine(ngrp, part):
-    members, _, nvol = part.shape
+    nvol = part.shape[2]
     return pl.pallas_call(
         functools.partial(combine_kernel, ngrp),
         out_shape=jax.ShapeDtypeStruct((7, nvol), F32),
         in_specs=[VMEM],
         out_specs=VMEM,
-        scratch_shapes=[
-            pltpu.VMEM((members, 8, nvol), F32),
-            pltpu.SemaphoreType.DMA((members,)),
-            pltpu.SemaphoreType.DMA((members,)),
-        ],
+        scratch_shapes=[pltpu.VMEM((ngrp, 8, nvol), F32)] * 3 + [pltpu.SemaphoreType.DMA((ngrp,))] * 4,
         compiler_params=pltpu.CompilerParams(collective_id=1, has_side_effects=True, vmem_limit_bytes=48 << 20),
     )(part)
 

time: 72.2 us -> 66.5 us (0.921)
  the two profiles are of different devices: /device:TPU:8 before, /device:TPU:17 now
where the time goes in v4:
time: 66.5 us; the launch traced here: 66.4 us
  Pallas kernels  65.1 us (98%)
  between operations  0.68 us (1%)
    pallas_call x1, Pallas kernels, blend(): pl.pallas_call(functools.partial(blend_kernel, ngrp, lmax), out_shape=jax...  34.2 us
    pallas_call x1, Pallas kernels, exchange(): pl.pallas_call(functools.partial(exchange_kernel, nchip, ngrp), out_shape...  23.4 us
    pallas_call x1, Pallas kernels, combine(): pl.pallas_call(functools.partial(combine_kernel, ngrp), out_shape=jax.Sha...  7.53 us

profile of v4, /device:TPU:17, one launch (start us, length us, event | category | flops | bytes accessed | tf_op | source)
XLA Modules:
  0.0 66.4 jit_solution(16110795778598274012)
XLA Ops:
  0.7 23.4 %shard_map.64 = (bf16[24,48,512]{2,1,0:T(8,128)(2,1)S(1)}, bf16[24,16,512]{2,1,0:T(8,128)(2,1)S(1)}, bf16[8,48,1024]{2,1,0:T(8,128)(2,1)S(1)}, s32[8,1,128]{2,1,0:T(1,128)S(1)}) custom-call(f32[3,4096]{1,0:T(4,128)} %pos_in.1, f32[7,4096]{1,0:T(8,128)} %mot_in.1, s32[32,128]{1,0:T(8,128)} %bitcast.1, f32[3,1024]{1,0:T(4,128)} %vol_in.1, s32[1,8]{1,0:T(1,128)} %infl_in.1, ...), custom_call_target="tpu_custom_call" | custom-call | tf_op jit(solution)/shard_map/pallas_call | solution.py:261
  24.0 34.2 %shard_map.65.part = f32[8,8,1024]{2,1,0:T(8,128)S(1)} custom-call(s32[8,1,128]{2,1,0:T(1,128)S(1)} %get-tuple-element.9.lists, bf16[24,48,512]{2,1,0:T(8,128)(2,1)S(1)} %get-tuple-element.10.fs, bf16[24,16,512]{2,1,0:T(8,128)(2,1)S(1)} %get-tuple-element.11.mt, bf16[8,48,1024]{2,1,0:T(8,128)(2,1)S(1)} %get-tuple-element.12.fv), custom_call_target="tpu_custom_call" | custom-call | tf_op jit(solution)/shard_map/pallas_call | solution.py:340
  58.2 7.5 %shard_map.66 = f32[7,1024]{1,0:T(8,128)S(1)} custom-call(f32[8,8,1024]{2,1,0:T(8,128)S(1)} %shard_map.65.part), custom_call_target="tpu_custom_call" | custom-call | tf_op jit(solution)/shard_map/pallas_call | solution.py:394
  65.8 0.6 copy.9

commit v5 on v4

--- a/solution.py
+++ b/solution.py
@@ -15,6 +15,7 @@
 ROWS = 10
 LANES = 128
 CORES = 2
+LATE = 2
 DEPTH = 48
 
 
@@ -289,8 +290,20 @@
     )(pos, mot, bins, vol, infl, cnt)
 
 
+def blended(fs, mt, fv, ns, js):
+    r2 = [dot(fs[n], fv[j], ((0,), (0,))) for n, j in zip(ns, js)]
+    sums = []
+    for n, d in zip(ns, r2):
+        w = pltpu.reciprocal(d * d, approx=True)
+        w1 = w.astype(BF16)
+        w2 = (w - w1.astype(F32)).astype(BF16)
+        m = mt[n]
+        sums.append(dot(m, w1) + dot(m, w2))
+    return sums
+
+
 def blend_kernel(ngrp, lmax, lists, fs, mt, fv, part, acc, block_of, bin_of):
-    q, _, _ = place()
+    q, _, x = place()
     members = fv.shape[0]
     base = (q - 1) * CORES * ngrp
 
@@ -302,20 +315,15 @@
             bin_of[filled] = lists[j, 0, l] - base
             return filled + 1
 
-        return lax.fori_loop(0, lists[j, 0, lmax], entry, filled)
+        return lax.fori_loop(jnp.where(j % ngrp == x, LATE, 0), lists[j, 0, lmax], entry, filled)
 
     total = lax.fori_loop(0, members, block, 0)
 
     def together(first, many):
         js = [block_of[first + k] for k in range(many)]
         ns = [bin_of[first + k] for k in range(many)]
-        r2 = [dot(fs[n], fv[j], ((0,), (0,))) for j, n in zip(js, ns)]
-        for j, n, d in zip(js, ns, r2):
-            w = pltpu.reciprocal(d * d, approx=True)
-            w1 = w.astype(BF16)
-            w2 = (w - w1.astype(F32)).astype(BF16)
-            m = mt[n]
-            acc[j] += dot(m, w1) + dot(m, w2)
+        for j, more in zip(js, blended(fs, mt, fv, ns, js)):
+            acc[j] += more
 
     def four(i, _):
         together(4 * i, 4)
@@ -351,8 +359,15 @@
     )(lists, fs, mt, fv)
 
 
-def combine_kernel(ngrp, part, out, across, along, sums, c_send, c_recv, x_send, x_recv):
+def combine_kernel(ngrp, lists, fs, mt, fv, part, out, across, along, sums, c_send, c_recv, x_send, x_recv):
     q, c, x = place()
+    base = (q - 1) * CORES * ngrp
+
+    def late(j):
+        ns = [jnp.clip(lists[j, 0, l] - base, 0, fs.shape[0] - 1) for l in range(LATE)]
+        more = sum(blended(fs, mt, fv, ns, [j] * LATE))
+        return part[j] + (more[:8] + more[8:])
+
     barrier = pltpu.get_barrier_semaphore()
     there = (q * CORES + 1 - c, x)
     pl.semaphore_signal(barrier, inc=1, device_id=there, device_id_type=MESH)
@@ -360,16 +375,17 @@
         pl.semaphore_signal(barrier, inc=1, device_id=(q * CORES + c, (x + o) % ngrp), device_id_type=MESH)
     pl.semaphore_wait(barrier, ngrp)
 
-    crossing = []
-    for o in (2, 1, 3, 0):
-        to = (x + o) % ngrp
+    def cross(to, src):
         copy = pltpu.make_async_remote_copy(
-            src_ref=part.at[(1 - c) * ngrp + to], dst_ref=across.at[to], send_sem=c_send.at[to], recv_sem=c_recv.at[to],
+            src_ref=src, dst_ref=across.at[to], send_sem=c_send.at[to], recv_sem=c_recv.at[to],
             device_id=there, device_id_type=MESH)
         copy.start()
-        crossing.append((o, to, copy))
+        return copy
+
+    others = [(o, (x + o) % ngrp) for o in (2, 1, 3)]
+    crossing = [cross(to, part.at[(1 - c) * ngrp + to]) for _, to in others]
     moving = []
-    for o, to, copy in crossing[:-1]:
+    for (o, to), copy in zip(others, crossing):
         copy.wait_recv()
         sums[o] = part[c * ngrp + to] + across[to]
         step = pltpu.make_async_remote_copy(
@@ -377,28 +393,32 @@
             device_id=(q * CORES + c, to), device_id_type=MESH)
         step.start()
         moving.append((o, step))
-    crossing[-1][2].wait_recv()
-    total = part[c * ngrp + x] + across[x]
+
+    sums[0] = late((1 - c) * ngrp + x)
+    last = cross(x, sums.at[0])
+    total = late(c * ngrp + x)
     for o, step in moving:
         step.wait_recv()
         total = total + along[o]
+    last.wait_recv()
+    total = total + across[x]
     out[...] = total[:7] / total[7:8]
-    for _, _, copy in crossing:
+    for copy in crossing + [last]:
         copy.wait_send()
     for _, step in moving:
         step.wait_send()
 
 
-def combine(ngrp, part):
+def combine(ngrp, lists, fs, mt, fv, part):
     nvol = part.shape[2]
     return pl.pallas_call(
         functools.partial(combine_kernel, ngrp),
         out_shape=jax.ShapeDtypeStruct((7, nvol), F32),
-        in_specs=[VMEM],
+        in_specs=[SMEM] + [VMEM] * 4,
         out_specs=VMEM,
         scratch_shapes=[pltpu.VMEM((ngrp, 8, nvol), F32)] * 3 + [pltpu.SemaphoreType.DMA((ngrp,))] * 4,
         compiler_params=pltpu.CompilerParams(collective_id=1, has_side_effects=True, vmem_limit_bytes=48 << 20),
-    )(part)
+    )(lists, fs, mt, fv, part)
 
 
 def on_device(surf_pos, surf_motion, surf_bin, vol_pos, influence, list_count):
@@ -409,7 +429,7 @@
         pltpu.with_memory_space_constraint(a, pltpu.HBM) for a in (surf_pos, surf_motion, bins, vol_pos, influence))
     fs, mt, fv, lists = exchange(nchip, ngrp, surf_pos, surf_motion, bins, vol_pos, influence, list_count)
     part = blend(ngrp, influence.shape[1], lists, fs, mt, fv)
-    return combine(ngrp, part)
+    return combine(ngrp, lists, fs, mt, fv, part)
 
 
 def solution(mesh):

time: 66.5 us -> 60.7 us (0.913)
  the two profiles are of different devices: /device:TPU:17 before, /device:TPU:49 now
where the time goes in v5:
time: 60.7 us; the launch traced here: 60.6 us
  Pallas kernels  59.3 us (98%)
  between operations  0.68 us (1%)
  local copies, waits for them, and re-layouts  0.62 us (1%)
    pallas_call x1, Pallas kernels, blend(): pl.pallas_call(functools.partial(blend_kernel, ngrp, lmax), out_shape=jax...  29.3 us
    pallas_call x1, Pallas kernels, exchange(): pl.pallas_call(functools.partial(exchange_kernel, nchip, ngrp), out_shape...  20.6 us
    pallas_call x1, Pallas kernels, combine(): pl.pallas_call(functools.partial(combine_kernel, ngrp), out_shape=jax.Sha...  9.45 us

profile of v5, /device:TPU:49, one launch (start us, length us, event | category | flops | bytes accessed | tf_op | source)
XLA Modules:
  0.0 60.6 jit_solution(1509527756155837194)
XLA Ops:
  0.7 20.6 %shard_map.64 = (bf16[24,48,512]{2,1,0:T(8,128)(2,1)S(1)}, bf16[24,16,512]{2,1,0:T(8,128)(2,1)S(1)}, bf16[8,48,1024]{2,1,0:T(8,128)(2,1)S(1)}, s32[8,1,128]{2,1,0:T(1,128)S(1)}) custom-call(f32[3,4096]{1,0:T(4,128)} %pos_in.1, f32[7,4096]{1,0:T(8,128)} %mot_in.1, s32[32,128]{1,0:T(8,128)} %bitcast.1, f32[3,1024]{1,0:T(4,128)} %vol_in.1, s32[1,8]{1,0:T(1,128)} %infl_in.1, ...), custom_call_target="tpu_custom_call" | custom-call | tf_op jit(solution)/shard_map/pallas_call | solution.py:262
  21.2 29.3 %shard_map.65.part = f32[8,8,1024]{2,1,0:T(8,128)S(1)} custom-call(s32[8,1,128]{2,1,0:T(1,128)S(1)} %get-tuple-element.9.lists, bf16[24,48,512]{2,1,0:T(8,128)(2,1)S(1)} %get-tuple-element.10.fs, bf16[24,16,512]{2,1,0:T(8,128)(2,1)S(1)} %get-tuple-element.11.mt, bf16[8,48,1024]{2,1,0:T(8,128)(2,1)S(1)} %get-tuple-element.12.fv), custom_call_target="tpu_custom_call" | custom-call | tf_op jit(solution)/shard_map/pallas_call | solution.py:348
  50.5 9.5 %shard_map.66 = f32[7,1024]{1,0:T(8,128)S(1)} custom-call(s32[8,1,128]{2,1,0:T(1,128)S(1)} %get-tuple-element.9.lists, bf16[24,48,512]{2,1,0:T(8,128)(2,1)S(1)} %get-tuple-element.10.fs, bf16[24,16,512]{2,1,0:T(8,128)(2,1)S(1)} %get-tuple-element.11.mt, bf16[8,48,1024]{2,1,0:T(8,128)(2,1)S(1)} %get-tuple-element.12.fv, f32[8,8,1024]{2,1,0:T(8,128)S(1)} %shard_map.65.part), custom_call_target="tpu_custom_call" | custom-call | tf_op jit(solution)/shard_map/pallas_call | solution.py:414
  60.0 0.6 %copy.9 = f32[7,1024]{1,0:T(8,128)} copy(f32[7,1024]{1,0:T(8,128)S(1)} %shard_map.66) | data formatting | bytes 57344
